TPU v7x, 256 devices: a whole 4x4x8 slice. The times are simulated.
256 devices in a mesh: dp: 32 (over x, z_lo, core), cent: 8 (over z_hi, y).
Axes of the slice: x: 4, y: 4, z: 8 (z_hi: 2, z_lo: 4; z = z_hi * 4 + z_lo), core: 2. Of those that a mesh axis runs over, the one named last changes fastest.
Arguments:
- embeddings: float32 [65536, 1024], P('dp'), may hold values from -100 to 100, as said below
- centroids: float32 [4096, 1024], P('cent'), may hold values from -5 to 5
- coarse_centroids: float32 [512, 1024], replicated, may hold values from -5 to 5
- top_centroids: float32 [64, 1024], replicated, may hold values from -5 to 5
Outputs:
- new_fine: float32 [8, 512, 1024], P('cent', 'dp')
- new_coarse: float32 [512, 1024], replicated
- new_top: float32 [64, 1024], replicated
Inputs may be any that keep to these rules, and one draw needn't show every extreme that they name: `embeddings`: embeddings are real-valued feature vectors.
All inputs are finite; a program needn't handle non-finite values.
Results may differ from a plain program's by a relative error of at most 0.0003.
Values sent between devices are 32-bit elements; how exact they have to be, the bound alone decides.
No kernel may reach another device: no remote copies, remote signals or barrier semaphores. Data moves between devices by JAX's collectives and lax.ppermute only.
A program may use at most 64 MiB of HBM per device.

v0:
```python
import jax
import jax.numpy as jnp
from jax import lax
from jax.sharding import PartitionSpec as P

epsilon = 1e-06
SHARPNESS = 1.5


def exact_dot(left, right, contract_left, contract_right):
    return lax.dot_general(
        left,
        right,
        (((contract_left,), (contract_right,)), ((), ())),
        precision=lax.Precision.HIGHEST,
        preferred_element_type=jnp.float32,
    )


def unit_rms(points):
    return points * lax.rsqrt(jnp.mean(points * points, axis=1, keepdims=True) + epsilon)


def center_logits(points, centers):
    inv_norm = lax.rsqrt(jnp.sum(centers * centers, axis=1) + epsilon)
    return SHARPNESS * exact_dot(points, centers, 1, 1) * inv_norm[None, :]


def local_fit(points, centers):
    logits = center_logits(points, centers)
    row_top = jnp.max(logits, axis=1)
    shifted = jnp.exp(logits - row_top[:, None])
    weights = shifted / jnp.sum(shifted, axis=1)[:, None]
    return (exact_dot(weights, points, 0, 0), jnp.sum(weights, axis=0))


def body(embeddings, centroids, coarse_centroids, top_centroids):
    logits = center_logits(embeddings, centroids)
    row_top = lax.pmax(jnp.max(logits, axis=1), "cent")
    shifted = jnp.exp(logits - row_top[:, None])
    row_total = lax.psum(jnp.sum(shifted, axis=1), "cent")
    weights = shifted / row_total[:, None]
    numerator = exact_dot(weights, embeddings, 0, 0)
    col_mass = jnp.sum(weights, axis=0)
    fine_sums, fine_mass = lax.psum((numerator, col_mass), "dp")
    fine_block = fine_sums / fine_mass[:, None]
    row_count = fine_block.shape[0] // lax.axis_size("dp")
    own_rows = lax.dynamic_slice_in_dim(fine_block, lax.axis_index("dp") * row_count, row_count, 0)
    coarse_part, coarse_part_mass = local_fit(unit_rms(fine_block), coarse_centroids)
    coarse_sums, coarse_mass = lax.psum((coarse_part, coarse_part_mass), "cent")
    new_coarse = coarse_sums / coarse_mass[:, None]
    top_sums, top_mass = local_fit(unit_rms(new_coarse), top_centroids)
    new_top = top_sums / top_mass[:, None]
    return (own_rows[None], new_coarse, new_top)


def solution(mesh):
    in_specs = (P("dp", None), P("cent", None), P(), P())
    out_specs = (P("cent", "dp", None), P(), P())
    return jax.shard_map(body, mesh=mesh, in_specs=in_specs, out_specs=out_specs, check_vma=False)
```

profile of v0, /device:TPU:1, one launch (start us, length us, event | category | flops | bytes accessed | tf_op | source)
XLA Modules:
  0.0 540.9 jit_solution(10748489473481135651)
XLA Ops:
  7.2 0.0 copy-start.3
  7.2 0.0 all-reduce.3.cloned.1.call-start
  7.2 1.9 multiply_reduce_fusion.4
  9.2 0.2 copy-done.3
  9.4 17.1 %multiply_reduce_fusion = (f32[2048]{0:T(1024)S(1)}, f32[2048,512]{0,1:T(8,128)}) fusion(f32[512]{0:T(512)S(1)} %rsqrt_multiply_fusion.1, f32[2048,1024]{1,0:T(8,128)} %param.4, f32[512,1024]{1,0:T(8,128)S(1)} %copy-done.3), kind=kOutput, calls=%fused_computation.1 | convolution fusion | flops 12886996992 | bytes 14690304 | tf_op jit(solution)/shard_map/dot_general | solution.py:11
  26.5 30.7 %pmax.7 = f32[2048]{0:T(1024)S(1)} all-reduce(f32[2048]{0:T(1024)S(1)} %get-tuple-element.7), channel_id=1, replica_groups=mesh['dp'=32,'cent'=8] {'cent'}, use_global_device_ids=true, to_apply=%region_2.0 | all-reduce | flops 2048 | bytes 16384 | tf_op jit(solution)/shard_map/pmax | solution.py:39
  57.2 2.9 fusion.1
  60.2 20.5 %psum.35 = f32[2048]{0:T(1024)S(1)} all-reduce(f32[2048]{0:T(1024)S(1)} %fusion.1), channel_id=1, replica_groups=mesh['dp'=32,'cent'=8] {'cent'}, use_global_device_ids=true, to_apply=%region_4.0 | all-reduce | flops 2048 | bytes 16384 | tf_op jit(solution)/shard_map/psum | solution.py:41
  80.7 17.9 %fusion.32 = f32[512,1024]{1,0:T(8,128)} fusion(f32[2048,1024]{1,0:T(8,128)} %param.4, f32[2048,512]{0,1:T(8,128)} %get-tuple-element.8, f32[2048]{0:T(1024)S(1)} %psum.35, f32[2048]{0:T(1024)S(1)} %pmax.7, f32[512]{0:T(512)S(1)} %rsqrt_multiply_fusion.1), kind=kOutput, calls=%fused_computation.41 | convolution fusion | flops 12888047616 | bytes 14698496 | tf_op jit(solution)/shard_map/dot_general | solution.py:11
  98.6 0.0 all-reduce.3.cloned.1.call-update
  98.6 0.0 copy-start.1
  98.6 0.2 all-reduce.5.cloned.1.call-start
  98.9 3.3 fusion.31
  102.1 74.8 %psum.37 = f32[512]{0:T(512)S(1)} all-reduce(f32[512]{0:T(512)S(1)} %fusion.31), channel_id=1, replica_groups=mesh['dp'=32,'cent'=8] {'dp'}, use_global_device_ids=true, to_apply=%region_7.0 | all-reduce | flops 512 | bytes 4096 | tf_op jit(solution)/shard_map/psum | solution.py:45
  177.0 0.0 copy-done.1
  177.0 0.2 multiply_reduce_fusion.2
  177.2 207.7 %all-reduce.3.cloned.1.call-done = f32[512,1024]{1,0:T(8,128)} async-done(((f32[512,1024]{1,0:T(8,128)}), f32[512,1024]{1,0:T(8,128)}) %all-reduce.3.cloned.1.call-update) | async-done | bytes 2097168 | tf_op jit(solution)/shard_map/psum | solution.py:45
  384.9 0.0 copy-start.2
  384.9 2.1 multiply_reduce_fusion.3
  387.1 0.1 copy-done.2
  387.2 3.7 fusion.34
  390.9 0.2 fusion.24
  391.1 5.1 fusion.6
  396.1 0.0 copy-start.4
  396.1 0.0 all-reduce.5.cloned.1.call-update
  396.2 0.9 copy-done.4
  397.1 0.1 multiply_reduce_fusion.5
  397.2 0.3 fusion.25
  397.5 27.3 %psum.39 = f32[512]{0:T(512)S(1)} all-reduce(f32[512]{0:T(512)S(1)} %fusion.25), channel_id=1, replica_groups=mesh['dp'=32,'cent'=8] {'cent'}, use_global_device_ids=true, to_apply=%region_14.0 | all-reduce | flops 512 | bytes 4096 | tf_op jit(solution)/shard_map/psum | solution.py:50
  424.7 0.6 dynamic-slice_bitcast_fusion
  425.4 101.9 %all-reduce.5.cloned.1.call-done = f32[512,1024]{1,0:T(8,128)} async-done(((f32[512,1024]{1,0:T(8,128)}), f32[512,1024]{1,0:T(8,128)}) %all-reduce.5.cloned.1.call-update) | async-done | bytes 2097168 | tf_op jit(solution)/shard_map/psum | solution.py:50
  527.3 2.0 multiply_reduce_fusion.1
  529.3 0.0 copy-start
  529.3 2.3 fusion.35
  531.6 0.1 fusion.29
  531.8 2.2 fusion.13
  534.0 0.0 copy-done
  (6 shorter events, 0.1 us)
Async XLA Ops:
  7.2 2.2 copy-start.3
  7.2 377.8 %all-reduce.3.cloned.1.call-start = ((), (), s32[]{:S(2)}) async-start(), calls=%async_computation | async-start | bytes 4194304 | tf_op jit(solution)/shard_map/psum | solution.py:45
  98.6 78.4 %copy-start.1 = (f32[512,1024]{1,0:T(8,128)S(1)}, f32[512,1024]{1,0:T(8,128)}, u32[]{:S(2)}) copy-start(f32[512,1024]{1,0:T(8,128)} %param.6) | copy-start | bytes 6291460
  98.6 428.7 %all-reduce.5.cloned.1.call-start = ((), (), s32[]{:S(2)}) async-start(), calls=%async_computation.1 | async-start | bytes 4194304 | tf_op jit(solution)/shard_map/psum | solution.py:50
  384.9 2.2 copy-start.2
  396.1 0.9 copy-start.4
  529.3 4.7 copy-start
Sparse Core Ops, SparseCore 0:
  98.7 286.1 all-reduce.2
  396.3 130.9 all-reduce.4
where the time goes:
time: 542 us; the launch traced here: 541 us
  waiting for transfers between devices  310 us (57%)
  blocking collectives  153 us (28%)
  matrix products  48.3 us (9%)
  between operations  14.1 us (3%)
  other arithmetic  13.2 us (2%)
    psum x1, waiting for transfers between devices, body(): fine_sums, fine_mass = lax.psum((numerator, col_mass), 'dp')  208 us
    psum x1, waiting for transfers between devices, body(): coarse_sums, coarse_mass = lax.psum((coarse_part, coarse_part_mass), 'cent')  102 us
    psum x1, blocking collectives, body(): fine_sums, fine_mass = lax.psum((numerator, col_mass), 'dp')  74.8 us
    dot_general x6, matrix products, exact_dot(): lax.dot_general(left, right, (((contract_left,), (contract_right,)), ((),...  48.3 us
    pmax x1, blocking collectives, body(): row_top = lax.pmax(jnp.max(logits, axis=1), 'cent')  30.7 us
    psum x1, blocking collectives, body(): coarse_sums, coarse_mass = lax.psum((coarse_part, coarse_part_mass), 'cent')  27.3 us
    psum x1, blocking collectives, body(): row_total = lax.psum(jnp.sum(shifted, axis=1), 'cent')  20.5 us
  transfers between devices with their start and end apart: 2, of which 2 were waited for; matrix products, arithmetic and copies ran while one was open for 1% of the time, Pallas kernels for 0%

commit v1 on v0

v1 whole, which is shorter than its diff:
```python
import jax
import jax.numpy as jnp
from jax import lax
from jax.sharding import Mesh, PartitionSpec as P

epsilon = 1e-06
SHARPNESS = 1.5
DP = ("x", "zl", "c")
CENT = ("zh", "y")
RING = ("zl", "zh", "y")
MASS = 128


def dot3(left, right, contract_left, contract_right):
    return lax.dot_general(
        left,
        right,
        (((contract_left,), (contract_right,)), ((), ())),
        precision=lax.Precision.HIGH,
        preferred_element_type=jnp.float32,
    )


def unit_rms(points):
    return points * lax.rsqrt(jnp.mean(points * points, axis=1, keepdims=True) + epsilon)


def center_logits(points, centers):
    inv_norm = lax.rsqrt(jnp.sum(centers * centers, axis=1) + epsilon)
    return SHARPNESS * dot3(points, centers, 1, 1) * inv_norm[None, :]


def softmax(logits):
    shifted = jnp.exp(logits - jnp.max(logits, axis=1, keepdims=True))
    return shifted / jnp.sum(shifted, axis=1, keepdims=True)


def spread(value, axes, size):
    return lax.all_to_all(jnp.broadcast_to(value[None], (size, *value.shape)), axes, 0, 0)


def with_mass(sums, mass):
    return jnp.concatenate([sums, jnp.broadcast_to(mass[:, None], (mass.shape[0], MASS))], axis=1)


def swap_core(value):
    return lax.ppermute(value, "c", [(0, 1), (1, 0)])


def body(embeddings, centroids, coarse_centroids, top_centroids):
    core = lax.axis_index("c")
    x = lax.axis_index("x")
    dim = embeddings.shape[1]
    centroids = centroids.reshape(4, 4, 2, 16, dim).transpose(2, 0, 1, 3, 4).reshape(512, dim)

    logits = center_logits(embeddings, centroids)
    own_top = jnp.max(logits, axis=1)
    shifted = jnp.exp(logits - own_top[:, None])
    own_total = jnp.sum(shifted, axis=1)
    stats = spread(jnp.stack([own_top, own_total]), CENT, 8)
    row_top = jnp.max(stats[:, 0], axis=0)
    row_total = jnp.sum(stats[:, 1] * jnp.exp(stats[:, 0] - row_top[None]), axis=0)
    weights = shifted * (jnp.exp(own_top - row_top) / row_total)[:, None]

    part = with_mass(dot3(weights, embeddings, 0, 0), jnp.sum(weights, axis=0))
    keep = lax.dynamic_slice_in_dim(part, core * 256, 256, 0)
    give = lax.dynamic_slice_in_dim(part, (1 - core) * 256, 256, 0)
    part = keep + swap_core(give)
    part = jnp.sum(lax.all_to_all(part.reshape(4, 64, dim + MASS), "x", 0, 0), axis=0)
    part = jnp.sum(lax.all_to_all(part.reshape(4, 16, dim + MASS), "zl", 0, 0), axis=0)
    fine = part[:, :dim] / part[:, dim : dim + 1]

    points = spread(unit_rms(fine), "x", 4).reshape(64, dim)
    points = jnp.concatenate([points, swap_core(points)], axis=0)
    weights = softmax(center_logits(points, coarse_centroids))
    weights = lax.dynamic_slice_in_dim(weights, (core * 4 + x) * 64, 64, 1)
    part = with_mass(dot3(weights, points, 0, 0), jnp.sum(weights, axis=0))
    part = jnp.sum(lax.all_to_all(part.reshape(32, 2, dim + MASS), RING, 0, 0), axis=0)
    coarse = part[:, :dim] / part[:, dim : dim + 1]
    coarse = spread(coarse, RING, 32).reshape(64, dim)
    coarse = spread(coarse, "x", 4).reshape(256, dim)
    other = swap_core(coarse)
    new_coarse = jnp.concatenate(
        [jnp.where(core == 0, coarse, other), jnp.where(core == 0, other, coarse)], axis=0
    )

    points = unit_rms(new_coarse)
    weights = softmax(center_logits(points, top_centroids))
    new_top = dot3(weights, points, 0, 0) / jnp.sum(weights, axis=0)[:, None]
    return (fine[None], new_coarse, new_top)


def solution(mesh):
    fold = Mesh(mesh.devices.reshape(4, 4, 2, 2, 4), DP + CENT)
    in_specs = (P(DP, None), P(CENT, None), P(), P())
    out_specs = (P(CENT, DP, None), P(), P())
    return jax.shard_map(body, mesh=fold, in_specs=in_specs, out_specs=out_specs, check_vma=False)
```

time: 542 us -> 159 us (0.29)
  waiting for transfers between devices: 310 us -> 15.1 us
  blocking collectives: 153 us -> 83.7 us
  matrix products: 48.3 us -> 24.7 us
  starting transfers between devices: 0.26 us -> 22.1 us
  between operations: 14.1 us -> 0.84 us
    psum x2 -> x0, waiting for transfers between devices: 310 us -> none  [the longest x1 208 us: body(): fine_sums, fine_mass = lax.psum((numerator, col_mass), 'dp')]
    psum x3 -> x0, blocking collectives: 123 us -> none  [the longest x1 74.8 us: body(): fine_sums, fine_mass = lax.psum((numerator, col_mass), 'dp')]
    all_to_all x0 -> x6, blocking collectives: none -> 83.7 us  [the longest x3 37.4 us: spread(): lax.all_to_all(jnp.broadcast_to(value[None], (size, *value.shape)), axes,...]
    pmax x1 -> x0, blocking collectives: 30.7 us -> none  [body(): row_top = lax.pmax(jnp.max(logits, axis=1), 'cent')]
    dot_general x6, matrix products: 48.3 us -> 24.7 us  [dot3(): lax.dot_general(left, right, (((contract_left,), (contract_right,)), ((),...]
    all_to_all x0 -> x1, starting transfers between devices: none -> 11.6 us  [spread(): lax.all_to_all(jnp.broadcast_to(value[None], (size, *value.shape)), axes,...]
    ppermute x0 -> x3, starting transfers between devices: none -> 10.4 us  [swap_core(): return lax.ppermute(value, 'c', [(0, 1), (1, 0)])]
    all_to_all x0 -> x1, waiting for transfers between devices: none -> 9.34 us  [spread(): lax.all_to_all(jnp.broadcast_to(value[None], (size, *value.shape)), axes,...]
  transfers between devices with their start and end apart: 2 -> 4, of which waited for: 2 -> 4; matrix products, arithmetic and copies ran while one was open for 1% -> 0% of each run, Pallas kernels for 0% -> 0%
where the time goes in v1:
time: 159 us; the launch traced here: 158 us
  blocking collectives  83.7 us (53%)
  matrix products  24.7 us (16%)
  starting transfers between devices  22.1 us (14%)
  waiting for transfers between devices  15.1 us (9%)
  other arithmetic  8.49 us (5%)
  local copies, waits for them, and re-layouts  3.4 us (2%)
    all_to_all x3, blocking collectives, spread(): lax.all_to_all(jnp.broadcast_to(value[None], (size, *value.shape)), axes,...  37.4 us
    dot_general x6, matrix products, dot3(): lax.dot_general(left, right, (((contract_left,), (contract_right,)), ((),...  24.7 us
    all_to_all x1, blocking collectives, body(): lax.all_to_all(part.reshape(4, 64, dim + MASS), 'x', 0, 0)  19.4 us
    all_to_all x1, blocking collectives, body(): lax.all_to_all(part.reshape(32, 2, dim + MASS), RING, 0, 0)  16 us
    all_to_all x1, starting transfers between devices, spread(): lax.all_to_all(jnp.broadcast_to(value[None], (size, *value.shape)), axes,...  11.6 us
    all_to_all x1, blocking collectives, body(): lax.all_to_all(part.reshape(4, 16, dim + MASS), 'zl', 0, 0)  10.9 us
    ppermute x3, starting transfers between devices, swap_core(): return lax.ppermute(value, 'c', [(0, 1), (1, 0)])  10.4 us
    all_to_all x1, waiting for transfers between devices, spread(): lax.all_to_all(jnp.broadcast_to(value[None], (size, *value.shape)), axes,...  9.34 us
  transfers between devices with their start and end apart: 4, of which 4 were waited for; matrix products, arithmetic and copies ran while one was open for 0% of the time, Pallas kernels for 0%

profile of v1, /device:TPU:1, one launch (start us, length us, event | category | flops | bytes accessed | tf_op | source)
XLA Modules:
  0.0 158.3 jit_solution(18033030403475920437)
XLA Ops:
  0.6 2.0 %multiply_reduce_fusion.4 = f32[2,4,4,16]{3,0,2,1:T(2,128)S(1)} fusion(f32[2,4,4,16,1024]{4,3,0,2,1:T(8,128)} %bitcast.31), kind=kLoop, calls=%fused_computation.16 | loop fusion | flops 1048064 | bytes 2099200 | tf_op jit(solution)/shard_map/reduce_sum | solution.py:29
  2.6 0.3 copy-done.3
  2.9 0.2 copy.24
  3.1 0.1 mul.102
  3.2 9.2 %multiply_reduce_fusion.1 = (f32[2048]{0:T(1024)S(1)}, f32[2048,512]{0,1:T(8,128)S(1)}) fusion(f32[512]{0:T(512)S(1)} %mul.102, f32[2048,1024]{1,0:T(8,128)} %param.4, f32[512,1024]{1,0:T(8,128)S(1)} %bitcast.33), kind=kOutput, calls=%fused_computation.4 | convolution fusion | flops 6444546048 | bytes 14690304 | tf_op jit(solution)/shard_map/dot_general | solution.py:15
  12.4 0.8 fusion.2
  13.2 1.1 copy-done
  14.4 0.7 broadcast_in_dim.16
  15.1 11.6 %all-to-all-start = ((f32[8,2,2048]{2,1,0:T(2,128)}), f32[8,2,2048]{2,1,0:T(2,128)S(1)}, u32[]{:S(2)}, u32[]{:S(2)}) async-start(f32[8,2,2048]{2,1,0:T(2,128)} %broadcast_in_dim.16), calls=%async_computation | async-start | bytes 262144 | tf_op jit(solution)/shard_map/all_to_all | solution.py:39
  26.7 9.3 %all-to-all-done = f32[8,2,2048]{2,1,0:T(2,128)S(1)} async-done(((f32[8,2,2048]{2,1,0:T(2,128)}), f32[8,2,2048]{2,1,0:T(2,128)S(1)}, u32[]{:S(2)}, u32[]{:S(2)}) %all-to-all-start) | async-done | bytes 131104 | tf_op jit(solution)/shard_map/all_to_all | solution.py:39
  36.1 0.1 slice_reduce_fusion.2
  36.3 11.1 %fusion = f32[512,1024]{1,0:T(8,128)S(1)} fusion(f32[2048,1024]{1,0:T(8,128)} %param.4, f32[2048,512]{0,1:T(8,128)} %copy-done, f32[2048]{0:T(1024)S(1)} %exponential_divide_fusion, f32[2048]{0:T(1024)S(1)} %get-tuple-element.14, f32[512]{0:T(512)S(1)} %mul.102), kind=kOutput, calls=%fused_computation.2 | convolution fusion | flops 6445596672 | bytes 14698496 | tf_op jit(solution)/shard_map/dot_general | solution.py:15
  47.4 1.0 multiply_reduce_fusion
  48.4 0.1 broadcast_in_dim.17
  48.5 1.1 fusion.10
  49.6 2.1 %collective-permute-start = (f32[256,1152]{1,0:T(8,128)}, f32[256,1152]{1,0:T(8,128)S(1)}, u32[]{:S(2)}, u32[]{:S(2)}) collective-permute-start(f32[256,1152]{1,0:T(8,128)} %fusion.10), channel_id=1, source_target_pairs={{0,8},{8,0},{1,9},{9,1},{2,10},{10,2},{3,11},{11,3},{4,12},{12,4},... | collective-permute-start | bytes 3538952 | tf_op jit(solution)/shard_map/ppermute | solution.py:47
  51.7 2.7 %collective-permute-done = f32[256,1152]{1,0:T(8,128)S(1)} collective-permute-done((f32[256,1152]{1,0:T(8,128)}, f32[256,1152]{1,0:T(8,128)S(1)}, u32[]{:S(2)}, u32[]{:S(2)}) %collective-permute-start) | collective-permute-done | bytes 1179680 | tf_op jit(solution)/shard_map/ppermute | solution.py:47
  54.4 0.1 fusion.12
  54.6 19.4 %all_to_all.35 = f32[4,64,1152]{2,1,0:T(8,128)S(1)} all-to-all(f32[4,64,1152]{2,1,0:T(8,128)S(1)} %bitcast.34), channel_id=1, replica_groups=mesh['x'=4,'zl'=4,'c'=2,'zh'=2,'y'=4] {'x'}, dimensions={0} | all-to-all | bytes 2359296 | tf_op jit(solution)/shard_map/all_to_all | solution.py:69
  74.0 0.8 reduce_sum.139
  74.8 10.9 %all_to_all.36 = f32[4,16,1152]{2,1,0:T(8,128)S(1)} all-to-all(f32[4,16,1152]{2,1,0:T(8,128)} %bitcast.39), channel_id=1, replica_groups=mesh['x'=4,'zl'=4,'c'=2,'zh'=2,'y'=4] {'zl'}, dimensions={0} | all-to-all | bytes 589824 | tf_op jit(solution)/shard_map/all_to_all | solution.py:70
  85.7 0.1 slice_reduce_fusion
  85.8 0.2 multiply_reduce_fusion.6
  86.0 0.7 broadcast_multiply_fusion
  86.7 7.9 %all_to_all.37 = f32[4,16,1024]{2,1,0:T(8,128)S(1)} all-to-all(f32[4,16,1024]{2,1,0:T(8,128)S(1)} %broadcast_in_dim.19), channel_id=1, replica_groups=mesh['x'=4,'zl'=4,'c'=2,'zh'=2,'y'=4] {'x'}, dimensions={0} | all-to-all | bytes 524288 | tf_op jit(solution)/shard_map/all_to_all | solution.py:39
  94.7 4.2 %collective-permute-start.1 = (f32[64,1024]{1,0:T(8,128)S(1)}, f32[64,1024]{1,0:T(8,128)S(1)}, u32[]{:S(2)}, u32[]{:S(2)}) collective-permute-start(f32[64,1024]{1,0:T(8,128)S(1)} %bitcast.36), channel_id=1, source_target_pairs={{0,8},{8,0},{1,9},{9,1},{2,10},{10,2},{3,11},{11,3},{4,12},{12,4},... | collective-permute-start | bytes 786440 | tf_op jit(solution)/shard_map/ppermute | solution.py:47
  98.9 0.2 multiply_reduce_fusion.3
  99.1 0.9 collective-permute-done.1
  100.1 1.3 fusion.38
  101.3 0.2 fusion.37
  101.5 0.1 fusion.32
  101.6 0.4 fusion.21
  102.2 0.2 reshape.91
  102.3 16.0 %all_to_all.38 = f32[32,2,1152]{2,1,0:T(2,128)S(1)} all-to-all(f32[32,2,1152]{2,1,0:T(2,128)S(1)} %reshape.91), channel_id=1, replica_groups=mesh['x'=4,'zl'=4,'c'=2,'zh'=2,'y'=4] {'zl','zh','y'}, dimensions={0} | all-to-all | bytes 589824 | tf_op jit(solution)/shard_map/all_to_all | solution.py:78
  118.3 0.1 reduce_sum.145
  118.4 0.1 slice_reduce_fusion.1
  118.7 15.1 %all_to_all.39 = f32[32,2,1024]{2,1,0:T(2,128)S(1)} all-to-all(f32[32,2,1024]{2,1,0:T(2,128)S(1)} %broadcast_in_dim.21), channel_id=1, replica_groups=mesh['x'=4,'zl'=4,'c'=2,'zh'=2,'y'=4] {'zl','zh','y'}, dimensions={0} | all-to-all | bytes 524288 | tf_op jit(solution)/shard_map/all_to_all | solution.py:39
  133.8 0.2 broadcast_in_dim.22
  134.0 0.1 broadcast_in_dim.23
  134.1 14.4 %all_to_all.40 = f32[4,64,1024]{2,1,0:T(8,128)S(1)} all-to-all(f32[4,64,1024]{2,1,0:T(8,128)S(1)} %broadcast_in_dim.23), channel_id=1, replica_groups=mesh['x'=4,'zl'=4,'c'=2,'zh'=2,'y'=4] {'x'}, dimensions={0} | all-to-all | bytes 2097152 | tf_op jit(solution)/shard_map/all_to_all | solution.py:39
  148.5 4.1 %collective-permute-start.2 = (f32[256,1024]{1,0:T(8,128)S(1)}, f32[256,1024]{1,0:T(8,128)S(1)}, u32[]{:S(2)}, u32[]{:S(2)}) collective-permute-start(f32[256,1024]{1,0:T(8,128)S(1)} %bitcast.35), channel_id=1, source_target_pairs={{0,8},{8,0},{1,9},{9,1},{2,10},{10,2},{3,11},{11,3},{4,12},{12,4},... | collective-permute-start | bytes 3145736 | tf_op jit(solution)/shard_map/ppermute | solution.py:47
  152.6 0.1 multiply_reduce_fusion.5
  152.7 2.2 %collective-permute-done.2 = f32[256,1024]{1,0:T(8,128)S(1)} collective-permute-done((f32[256,1024]{1,0:T(8,128)S(1)}, f32[256,1024]{1,0:T(8,128)S(1)}, u32[]{:S(2)}, u32[]{:S(2)}) %collective-permute-start.2) | collective-permute-done | bytes 1048608 | tf_op jit(solution)/shard_map/ppermute | solution.py:47
  154.8 0.2 broadcast_select_fusion.1
  155.1 0.3 multiply_reduce_fusion.2
  155.4 1.2 fusion.39
  156.6 0.1 fusion.28
  156.8 1.5 fusion.13
  (25 shorter events, 0.5 us)
Async XLA Ops:
  0.6 2.2 %copy-start.3 = (f32[512,1024]{1,0:T(8,128)S(1)}, f32[512,1024]{1,0:T(8,128)}, u32[]{:S(2)}) copy-start(f32[512,1024]{1,0:T(8,128)} %param.5) | copy-start | bytes 6291460
  12.4 1.9 %copy-start = (f32[2048,512]{0,1:T(8,128)}, f32[2048,512]{0,1:T(8,128)S(1)}, u32[]{:S(2)}) copy-start(f32[2048,512]{0,1:T(8,128)S(1)} %get-tuple-element.15) | copy-start | bytes 12582916
  15.1 21.0 %all-to-all-start = ((f32[8,2,2048]{2,1,0:T(2,128)}), f32[8,2,2048]{2,1,0:T(2,128)S(1)}, u32[]{:S(2)}, u32[]{:S(2)}) async-start(f32[8,2,2048]{2,1,0:T(2,128)} %broadcast_in_dim.16), calls=%async_computation | async-start | bytes 262144 | tf_op jit(solution)/shard_map/all_to_all | solution.py:39
  36.3 11.1 %copy-start.1 = (f32[2048,512]{0,1:T(8,128)S(1)}, f32[2048,512]{0,1:T(8,128)}, u32[]{:S(2)}) copy-start(f32[2048,512]{0,1:T(8,128)} %copy-done) | copy-start | bytes 12582916
  49.6 4.8 %collective-permute-start = (f32[256,1152]{1,0:T(8,128)}, f32[256,1152]{1,0:T(8,128)S(1)}, u32[]{:S(2)}, u32[]{:S(2)}) collective-permute-start(f32[256,1152]{1,0:T(8,128)} %fusion.10), channel_id=1, source_target_pairs={{0,8},{8,0},{1,9},{9,1},{2,10},{10,2},{3,11},{11,3},{4,12},{12,4},... | collective-permute-start | bytes 3538952 | tf_op jit(solution)/shard_map/ppermute | solution.py:47
  74.0 24.9 %copy-start.4 = (f32[512,1024]{1,0:T(8,128)S(1)}, f32[512,1024]{1,0:T(8,128)}, u32[]{:S(2)}) copy-start(f32[512,1024]{1,0:T(8,128)} %param.6) | copy-start | bytes 6291460
  94.7 5.4 %collective-permute-start.1 = (f32[64,1024]{1,0:T(8,128)S(1)}, f32[64,1024]{1,0:T(8,128)S(1)}, u32[]{:S(2)}, u32[]{:S(2)}) collective-permute-start(f32[64,1024]{1,0:T(8,128)S(1)} %bitcast.36), channel_id=1, source_target_pairs={{0,8},{8,0},{1,9},{9,1},{2,10},{10,2},{3,11},{11,3},{4,12},{12,4},... | collective-permute-start | bytes 786440 | tf_op jit(solution)/shard_map/ppermute | solution.py:47
  133.8 18.8 %copy-start.5 = (f32[64,1024]{1,0:T(8,128)S(1)}, f32[64,1024]{1,0:T(8,128)}, u32[]{:S(2)}) copy-start(f32[64,1024]{1,0:T(8,128)} %param.7) | copy-start | bytes 786436
  148.5 6.4 %collective-permute-start.2 = (f32[256,1024]{1,0:T(8,128)S(1)}, f32[256,1024]{1,0:T(8,128)S(1)}, u32[]{:S(2)}, u32[]{:S(2)}) collective-permute-start(f32[256,1024]{1,0:T(8,128)S(1)} %bitcast.35), channel_id=1, source_target_pairs={{0,8},{8,0},{1,9},{9,1},{2,10},{10,2},{3,11},{11,3},{4,12},{12,4},... | collective-permute-start | bytes 3145736 | tf_op jit(solution)/shard_map/ppermute | solution.py:47
  155.4 2.9 %copy-start.2 = (f32[512,1024]{1,0:T(8,128)}, f32[512,1024]{1,0:T(8,128)S(1)}, u32[]{:S(2)}) copy-start(f32[512,1024]{1,0:T(8,128)S(1)} %get-tuple-element.4) | copy-start | bytes 6291460

commit v2 on v1

v2 whole, which is shorter than its diff:
```python
import functools

import jax
import jax.numpy as jnp
from jax import lax
from jax.experimental import pallas as pl
from jax.experimental.pallas import tpu as pltpu
from jax.sharding import Mesh, PartitionSpec as P

epsilon = 1e-06
SHARPNESS = 1.5
DP = ("x", "zl", "c")
CENT = ("zh", "y")
MASS = 128
F32, BF16 = jnp.float32, jnp.bfloat16
VMEM = 24 * 2**20
NT = (((1,), (1,)), ((), ()))
NN = (((1,), (0,)), ((), ()))


def split(value):
    high = value.astype(BF16)
    return high, (value - high.astype(F32)).astype(BF16)


def mm(left, right, dims):
    return lax.dot_general(left, right, dims, preferred_element_type=F32)


def fit_kernel(step, e_ref, c_ref, p_ref, stat_ref, eh_ref, el_ref, ch, cl):
    @pl.when(pl.program_id(0) == 0)
    def _():
        c = c_ref[...]
        c = c * (SHARPNESS * lax.rsqrt(jnp.sum(c * c, axis=1, keepdims=True) + epsilon))
        high, low = split(c)
        for chip in range(16):
            for core in range(2):
                here, there = (chip * 2 + core) * 16, (core * 16 + chip) * 16
                ch[there : there + 16, :] = high[here : here + 16, :]
                cl[there : there + 16, :] = low[here : here + 16, :]

    for j in range(0, e_ref.shape[0], step):
        rows = slice(j, j + step)
        eh, el = split(e_ref[rows, :])
        eh_ref[rows, :] = eh
        el_ref[rows, :] = el
        logits = mm(ch[...], eh, NT) + mm(ch[...], el, NT) + mm(cl[...], eh, NT)
        top = jnp.max(logits, axis=0, keepdims=True)
        p = jnp.exp(logits - top)
        p_ref[:, rows] = p
        stat_ref[0:1, rows] = top
        stat_ref[1:2, rows] = jnp.sum(p, axis=0, keepdims=True)


def fit(e, c, block=512, step=256):
    (n, d), k = e.shape, c.shape[0]
    return pl.pallas_call(
        functools.partial(fit_kernel, step),
        grid=(n // block,),
        in_specs=[pl.BlockSpec((block, d), lambda i: (i, 0)), pl.BlockSpec((k, d), lambda i: (0, 0))],
        out_specs=[
            pl.BlockSpec((k, block), lambda i: (0, i)),
            pl.BlockSpec((2, block), lambda i: (0, i)),
            pl.BlockSpec((block, d), lambda i: (i, 0)),
            pl.BlockSpec((block, d), lambda i: (i, 0)),
        ],
        out_shape=[
            jax.ShapeDtypeStruct((k, n), F32),
            jax.ShapeDtypeStruct((2, n), F32),
            jax.ShapeDtypeStruct((n, d), BF16),
            jax.ShapeDtypeStruct((n, d), BF16),
        ],
        scratch_shapes=[pltpu.VMEM((k, d), BF16)] * 2,
        compiler_params=pltpu.CompilerParams(vmem_limit_bytes=VMEM),
        name="fit",
    )(e, c)


def sums_kernel(_, stats_ref, own_ref, p_ref, eh_ref, el_ref, o_ref):
    @pl.when(pl.program_id(0) == 0)
    def _():
        o_ref[...] = jnp.zeros_like(o_ref)

    tops, totals = stats_ref[:, 0, :], stats_ref[:, 1, :]
    top = jnp.max(tops, axis=0, keepdims=True)
    total = jnp.sum(totals * jnp.exp(tops - top), axis=0, keepdims=True)
    w = p_ref[...] * (jnp.exp(own_ref[0:1, :] - top) / total)
    wh, wl = split(w)
    d = eh_ref.shape[1]
    o_ref[:, d:] += jnp.broadcast_to(jnp.sum(w, axis=1, keepdims=True), (w.shape[0], MASS))
    o_ref[:, :d] += mm(wh, eh_ref[...], NN) + mm(wh, el_ref[...], NN) + mm(wl, eh_ref[...], NN)


def sums(stats, own, p, eh, el, half, block=1024):
    n, d = eh.shape
    k = p.shape[0] // 2
    return pl.pallas_call(
        sums_kernel,
        grid_spec=pltpu.PrefetchScalarGridSpec(
            num_scalar_prefetch=1,
            grid=(n // block,),
            in_specs=[
                pl.BlockSpec((8, 2, block), lambda i, half: (0, 0, i)),
                pl.BlockSpec((2, block), lambda i, half: (0, i)),
                pl.BlockSpec((k, block), lambda i, half: (half[0], i)),
                pl.BlockSpec((block, d), lambda i, half: (i, 0)),
                pl.BlockSpec((block, d), lambda i, half: (i, 0)),
            ],
            out_specs=pl.BlockSpec((k, d + MASS), lambda i, half: (0, 0)),
        ),
        out_shape=jax.ShapeDtypeStruct((k, d + MASS), F32),
        compiler_params=pltpu.CompilerParams(vmem_limit_bytes=VMEM),
        cost_estimate=pl.CostEstimate(flops=6 * n * d * k, bytes_accessed=12 * n * k, transcendentals=0),
        name="sums",
    )(half, stats, own, p, eh, el)


def dot3(left, right, contract_left, contract_right):
    return lax.dot_general(
        left,
        right,
        (((contract_left,), (contract_right,)), ((), ())),
        precision=lax.Precision.HIGH,
        preferred_element_type=F32,
    )


def unit_rms(points):
    return points * lax.rsqrt(jnp.mean(points * points, axis=1, keepdims=True) + epsilon)


def center_logits(points, centers):
    inv_norm = lax.rsqrt(jnp.sum(centers * centers, axis=1) + epsilon)
    return SHARPNESS * dot3(points, centers, 1, 1) * inv_norm[None, :]


def softmax(logits):
    shifted = jnp.exp(logits - jnp.max(logits, axis=1, keepdims=True))
    return shifted / jnp.sum(shifted, axis=1, keepdims=True)


def spread(value, axes, size):
    return lax.all_to_all(jnp.broadcast_to(value[None], (size, *value.shape)), axes, 0, 0)


def add_up(part, axes, size):
    part = part.reshape(size, part.shape[0] // size, part.shape[1])
    return jnp.sum(lax.all_to_all(part, axes, 0, 0), axis=0)


def with_mass(sums, mass):
    return jnp.concatenate([sums, jnp.broadcast_to(mass[:, None], (mass.shape[0], MASS))], axis=1)


def swap_core(value):
    return lax.ppermute(value, "c", [(0, 1), (1, 0)])


def body(embeddings, centroids, coarse_centroids, top_centroids):
    core = lax.axis_index("c")
    dim = embeddings.shape[1]
    embeddings, centroids = (pltpu.with_memory_space_constraint(a, pltpu.HBM) for a in (embeddings, centroids))
    p, own, eh, el = fit(embeddings, centroids)
    mine, theirs = core.reshape(1), 1 - core.reshape(1)
    own, mine, theirs = lax.optimization_barrier((own, mine, theirs))
    stats = spread(own, CENT, 8)
    part = swap_core(sums(stats, own, p, eh, el, theirs)) + sums(stats, own, p, eh, el, mine)
    part = add_up(add_up(part, "x", 4), "zl", 4)
    fine = part[:, :dim] / part[:, dim : dim + 1]

    points = spread(unit_rms(fine), "x", 4).reshape(64, dim)
    points = jnp.concatenate([points, swap_core(points)], axis=0)
    weights = softmax(center_logits(points, coarse_centroids))
    weights = lax.dynamic_slice_in_dim(weights, (core * 4 + lax.axis_index("x")) * 64, 64, 1)
    part = with_mass(dot3(weights, points, 0, 0), jnp.sum(weights, axis=0))
    part = add_up(part, ("y", "zh", "zl"), 32)
    coarse = part[:, :dim] / part[:, dim : dim + 1]
    coarse = spread(coarse, ("zh", "zl"), 8).reshape(16, dim)
    coarse = spread(coarse, ("x", "y"), 16).reshape(256, dim)
    other = swap_core(coarse)
    new_coarse = jnp.concatenate(
        [jnp.where(core == 0, coarse, other), jnp.where(core == 0, other, coarse)], axis=0
    )

    points = unit_rms(new_coarse)
    weights = softmax(center_logits(points, top_centroids))
    new_top = dot3(weights, points, 0, 0) / jnp.sum(weights, axis=0)[:, None]
    return (fine[None], new_coarse, new_top)


def solution(mesh):
    fold = Mesh(mesh.devices.reshape(4, 4, 2, 2, 4), DP + CENT)
    in_specs = (P(DP, None), P(CENT, None), P(), P())
    out_specs = (P(CENT, DP, None), P(), P())
    return jax.shard_map(body, mesh=fold, in_specs=in_specs, out_specs=out_specs, check_vma=False)
```

time: 159 us -> 145 us (0.912)
  matrix products: 24.7 us -> 4.38 us
  Pallas kernels: 0 us -> 19.1 us
  blocking collectives: 83.7 us -> 102 us
  waiting for transfers between devices: 15.1 us -> 3.09 us
  starting transfers between devices: 22.1 us -> 11.3 us
  other arithmetic: 8.49 us -> 3.44 us
  local copies, waits for them, and re-layouts: 3.4 us -> 0.72 us
    all_to_all x3 -> x4, blocking collectives: 37.4 us -> 57.9 us  [spread(): lax.all_to_all(jnp.broadcast_to(value[None], (size, *value.shape)), axes,...]
    dot_general x6 -> x4, matrix products: 24.7 us -> 4.38 us  [dot3(): lax.dot_general(left, right, (((contract_left,), (contract_right,)), ((),...]
    pallas_call x0 -> x3, Pallas kernels: none -> 19.1 us  [the longest x1 11.3 us: fit(): pl.pallas_call(functools.partial(fit_kernel, step), grid=(n // block,), i...]
    all_to_all x1 -> x0, starting transfers between devices: 11.6 us -> none  [spread(): lax.all_to_all(jnp.broadcast_to(value[None], (size, *value.shape)), axes,...]
    all_to_all x1 -> x0, waiting for transfers between devices: 9.34 us -> none  [spread(): lax.all_to_all(jnp.broadcast_to(value[None], (size, *value.shape)), axes,...]
    ppermute x3, waiting for transfers between devices: 5.78 us -> 3.09 us  [swap_core(): return lax.ppermute(value, 'c', [(0, 1), (1, 0)])]
    all_to_all x3, blocking collectives: 46.3 us -> 44.2 us  [add_up(): return jnp.sum(lax.all_to_all(part, axes, 0, 0), axis=0)]
    reduce_sum x3 -> x2, other arithmetic: 2.29 us -> 0.33 us  [center_logits(): inv_norm = lax.rsqrt(jnp.sum(centers * centers, axis=1) + epsilon)]
  transfers between devices with their start and end apart: 4 -> 3, of which waited for: 4 -> 2; matrix products, arithmetic and copies ran while one was open for 0% -> 0% of each run, Pallas kernels for 0% -> 3%
where the time goes in v2:
time: 145 us
  blocking collectives  102 us (70%)
  Pallas kernels  19.1 us (13%)
  starting transfers between devices  11.3 us (8%)
  matrix products  4.38 us (3%)
  other arithmetic  3.44 us (2%)
  waiting for transfers between devices  3.09 us (2%)
    all_to_all x4, blocking collectives, spread(): lax.all_to_all(jnp.broadcast_to(value[None], (size, *value.shape)), axes,...  57.9 us
    all_to_all x3, blocking collectives, add_up(): return jnp.sum(lax.all_to_all(part, axes, 0, 0), axis=0)  44.2 us
    pallas_call x1, Pallas kernels, fit(): pl.pallas_call(functools.partial(fit_kernel, step), grid=(n // block,), i...  11.3 us
    ppermute x3, starting transfers between devices, swap_core(): return lax.ppermute(value, 'c', [(0, 1), (1, 0)])  11.3 us
    pallas_call x2, Pallas kernels, sums(): pl.pallas_call(sums_kernel, grid_spec=pltpu.PrefetchScalarGridSpec(num_sc...  7.76 us
    dot_general x4, matrix products, dot3(): lax.dot_general(left, right, (((contract_left,), (contract_right,)), ((),...  4.38 us
    ppermute x3, waiting for transfers between devices, swap_core(): return lax.ppermute(value, 'c', [(0, 1), (1, 0)])  3.09 us
  transfers between devices with their start and end apart: 3, of which 2 were waited for; matrix products, arithmetic and copies ran while one was open for 0% of the time, Pallas kernels for 3%

profile of v2, /device:TPU:1, one launch (start us, length us, event | category | flops | bytes accessed | tf_op | source)
XLA Modules:
  0.0 145.0 jit_solution(4505240307707632340)
XLA Ops:
  0.6 11.3 %fit.1 = (f32[512,2048]{1,0:T(8,128)S(1)}, f32[2,2048]{1,0:T(2,128)S(1)}, bf16[2048,1024]{1,0:T(8,128)(2,1)S(1)}, bf16[2048,1024]{1,0:T(8,128)(2,1)S(1)}) custom-call(f32[2048,1024]{1,0:T(8,128)} %e_ref.1, f32[512,1024]{1,0:T(8,128)} %c_ref.1), custom_call_target="tpu_custom_call" | custom-call | tf_op jit(solution)/shard_map/fit/pallas_call | solution.py:57
  12.0 20.8 %all_to_all.35.stats_ref = f32[8,2,2048]{2,1,0:T(2,128)S(1)} all-to-all(f32[8,2,2048]{2,1,0:T(2,128)S(1)} %broadcast_in_dim.14), channel_id=1, replica_groups=mesh['x'=4,'zl'=4,'c'=2,'zh'=2,'y'=4] {'zh','y'}, dimensions={0} | all-to-all | bytes 262144 | tf_op jit(solution)/shard_map/all_to_all | solution.py:143
  32.8 3.9 %sums.2 = f32[256,1152]{1,0:T(8,128)S(1)} custom-call(s32[1]{0:T(128)S(6)} %sub.19._, f32[8,2,2048]{2,1,0:T(2,128)S(1)} %all_to_all.35.stats_ref, f32[2,2048]{1,0:T(2,128)S(1)} %get-tuple-element.12.own_ref, f32[512,2048]{1,0:T(8,128)S(1)} %get-tuple-element.13.p_ref, bf16[2048,1024]{1,0:T(8,128)(2,1)S(1)} %get-tuple-element.14.eh_ref, ...), custom_call_target="tpu_custom_call" | custom-call | flops 3221225472 | bytes 6291456 | tf_op jit(solution)/shard_map/sums/pallas_call | solution.py:97
  36.7 2.2 %collective-permute-start = (f32[256,1152]{1,0:T(8,128)S(1)}, f32[256,1152]{1,0:T(8,128)S(1)}, u32[]{:S(2)}, u32[]{:S(2)}) collective-permute-start(f32[256,1152]{1,0:T(8,128)S(1)} %sums.2), channel_id=1, source_target_pairs={{0,8},{8,0},{1,9},{9,1},{2,10},{10,2},{3,11},{11,3},{4,12},{12,4},... | collective-permute-start | bytes 3538952 | tf_op jit(solution)/shard_map/ppermute | solution.py:156
  38.9 3.9 %sums.3 = f32[256,1152]{1,0:T(8,128)S(1)} custom-call(s32[1]{0:T(128)} %bitcast._, f32[8,2,2048]{2,1,0:T(2,128)S(1)} %all_to_all.35.stats_ref, f32[2,2048]{1,0:T(2,128)S(1)} %get-tuple-element.12.own_ref, f32[512,2048]{1,0:T(8,128)S(1)} %get-tuple-element.13.p_ref, bf16[2048,1024]{1,0:T(8,128)(2,1)S(1)} %get-tuple-element.14.eh_ref, ...), custom_call_target="tpu_custom_call" | custom-call | flops 3221225472 | bytes 6291456 | tf_op jit(solution)/shard_map/sums/pallas_call | solution.py:97
  42.8 0.0 collective-permute-done
  42.8 0.1 add.46
  42.9 20.1 %all_to_all.36 = f32[4,64,1152]{2,1,0:T(8,128)S(1)} all-to-all(f32[4,64,1152]{2,1,0:T(8,128)S(1)} %bitcast.11), channel_id=1, replica_groups=mesh['x'=4,'zl'=4,'c'=2,'zh'=2,'y'=4] {'x'}, dimensions={0} | all-to-all | bytes 2359296 | tf_op jit(solution)/shard_map/all_to_all | solution.py:148
  63.0 0.0 copy-start.1
  63.0 0.8 reduce_sum.99
  63.8 10.6 %all_to_all.37 = f32[4,16,1152]{2,1,0:T(8,128)S(1)} all-to-all(f32[4,16,1152]{2,1,0:T(8,128)} %bitcast.16), channel_id=1, replica_groups=mesh['x'=4,'zl'=4,'c'=2,'zh'=2,'y'=4] {'zl'}, dimensions={0} | all-to-all | bytes 589824 | tf_op jit(solution)/shard_map/all_to_all | solution.py:148
  74.5 0.1 slice_reduce_fusion
  74.6 0.2 multiply_reduce_fusion.3
  74.8 0.7 broadcast_multiply_fusion
  75.5 7.9 %all_to_all.38 = f32[4,16,1024]{2,1,0:T(8,128)S(1)} all-to-all(f32[4,16,1024]{2,1,0:T(8,128)S(1)} %broadcast_in_dim.16), channel_id=1, replica_groups=mesh['x'=4,'zl'=4,'c'=2,'zh'=2,'y'=4] {'x'}, dimensions={0} | all-to-all | bytes 524288 | tf_op jit(solution)/shard_map/all_to_all | solution.py:143
  83.5 4.5 %collective-permute-start.1 = (f32[64,1024]{1,0:T(8,128)S(1)}, f32[64,1024]{1,0:T(8,128)S(1)}, u32[]{:S(2)}, u32[]{:S(2)}) collective-permute-start(f32[64,1024]{1,0:T(8,128)S(1)} %bitcast.13), channel_id=1, source_target_pairs={{0,8},{8,0},{1,9},{9,1},{2,10},{10,2},{3,11},{11,3},{4,12},{12,4},... | collective-permute-start | bytes 786440 | tf_op jit(solution)/shard_map/ppermute | solution.py:156
  87.9 0.0 copy-done.1
  87.9 0.2 multiply_reduce_fusion.1
  88.2 0.9 collective-permute-done.1
  89.1 1.3 fusion.23
  90.4 0.2 fusion.22
  90.6 0.1 fusion.17
  90.7 0.4 fusion.12
  91.1 0.1 broadcast_in_dim.17
  91.2 0.2 reshape.63
  91.4 0.0 copy-start.2
  91.4 13.5 %all_to_all.39 = f32[32,2,1152]{2,1,0:T(2,128)S(1)} all-to-all(f32[32,2,1152]{2,1,0:T(2,128)S(1)} %reshape.63), channel_id=1, replica_groups=mesh['x'=4,'zl'=4,'c'=2,'zh'=2,'y'=4] {'y','zh','zl'}, dimensions={0} | all-to-all | bytes 589824 | tf_op jit(solution)/shard_map/all_to_all | solution.py:148
  104.9 0.1 reduce_sum.105
  105.0 0.1 slice_reduce_fusion.1
  105.1 0.1 slice_divide_fusion.1
  105.2 12.0 %all_to_all.40 = f32[8,2,1024]{2,1,0:T(2,128)S(1)} all-to-all(f32[8,2,1024]{2,1,0:T(2,128)S(1)} %broadcast_in_dim.18), channel_id=1, replica_groups=mesh['x'=4,'zl'=4,'c'=2,'zh'=2,'y'=4] {'zh','zl'}, dimensions={0} | all-to-all | bytes 131072 | tf_op jit(solution)/shard_map/all_to_all | solution.py:143
  117.3 0.1 broadcast_in_dim.20
  117.4 17.2 %all_to_all.41 = f32[16,16,1024]{2,1,0:T(8,128)S(1)} all-to-all(f32[16,16,1024]{2,1,0:T(8,128)S(1)} %broadcast_in_dim.20), channel_id=1, replica_groups=mesh['x'=4,'zl'=4,'c'=2,'zh'=2,'y'=4] {'x','y'}, dimensions={0} | all-to-all | bytes 2097152 | tf_op jit(solution)/shard_map/all_to_all | solution.py:143
  134.6 4.6 %collective-permute-start.2 = (f32[256,1024]{1,0:T(8,128)S(1)}, f32[256,1024]{1,0:T(8,128)S(1)}, u32[]{:S(2)}, u32[]{:S(2)}) collective-permute-start(f32[256,1024]{1,0:T(8,128)S(1)} %bitcast.12), channel_id=1, source_target_pairs={{0,8},{8,0},{1,9},{9,1},{2,10},{10,2},{3,11},{11,3},{4,12},{12,4},... | collective-permute-start | bytes 3145736 | tf_op jit(solution)/shard_map/ppermute | solution.py:156
  139.2 0.0 copy-done.2
  139.2 0.1 multiply_reduce_fusion.2
  139.4 2.2 %collective-permute-done.2 = f32[256,1024]{1,0:T(8,128)S(1)} collective-permute-done((f32[256,1024]{1,0:T(8,128)S(1)}, f32[256,1024]{1,0:T(8,128)S(1)}, u32[]{:S(2)}, u32[]{:S(2)}) %collective-permute-start.2) | collective-permute-done | bytes 1048608 | tf_op jit(solution)/shard_map/ppermute | solution.py:156
  141.5 0.2 broadcast_select_fusion.1
  141.7 0.3 multiply_reduce_fusion
  142.1 0.0 copy-start
  142.1 1.2 fusion.24
  143.3 0.1 fusion.15
  143.4 1.6 %fusion.4 = f32[64,1024]{1,0:T(8,128)} fusion(f32[512,1024]{1,0:T(8,128)S(1)} %get-tuple-element.18, f32[512]{0:T(512)S(1)} %add_rsqrt_fusion, f32[64]{0:T(128)S(1)} %fusion.15, f32[512,64]{0,1:T(8,128)S(1)} %get-tuple-element.28, f32[512]{0:T(512)S(1)} %fusion.14, f32[512]{0:T(512)S(1)} %get-tuple-element.27), kind=kOutput, calls=%fused_computation.7 | convolution fusion | flops 201981952 | bytes 2496768 | tf_op jit(solution)/shard_map/dot_general | solution.py:119
  145.0 0.0 copy-done
  (11 shorter events, 0.2 us)
Async XLA Ops:
  36.7 6.1 %collective-permute-start = (f32[256,1152]{1,0:T(8,128)S(1)}, f32[256,1152]{1,0:T(8,128)S(1)}, u32[]{:S(2)}, u32[]{:S(2)}) collective-permute-start(f32[256,1152]{1,0:T(8,128)S(1)} %sums.2), channel_id=1, source_target_pairs={{0,8},{8,0},{1,9},{9,1},{2,10},{10,2},{3,11},{11,3},{4,12},{12,4},... | collective-permute-start | bytes 3538952 | tf_op jit(solution)/shard_map/ppermute | solution.py:156
  63.0 24.9 %copy-start.1 = (f32[512,1024]{1,0:T(8,128)S(1)}, f32[512,1024]{1,0:T(8,128)}, u32[]{:S(2)}) copy-start(f32[512,1024]{1,0:T(8,128)} %param.6) | copy-start | bytes 6291460
  83.5 5.6 %collective-permute-start.1 = (f32[64,1024]{1,0:T(8,128)S(1)}, f32[64,1024]{1,0:T(8,128)S(1)}, u32[]{:S(2)}, u32[]{:S(2)}) collective-permute-start(f32[64,1024]{1,0:T(8,128)S(1)} %bitcast.13), channel_id=1, source_target_pairs={{0,8},{8,0},{1,9},{9,1},{2,10},{10,2},{3,11},{11,3},{4,12},{12,4},... | collective-permute-start | bytes 786440 | tf_op jit(solution)/shard_map/ppermute | solution.py:156
  91.4 47.9 %copy-start.2 = (f32[64,1024]{1,0:T(8,128)S(1)}, f32[64,1024]{1,0:T(8,128)}, u32[]{:S(2)}) copy-start(f32[64,1024]{1,0:T(8,128)} %param.7) | copy-start | bytes 786436
  134.6 6.9 %collective-permute-start.2 = (f32[256,1024]{1,0:T(8,128)S(1)}, f32[256,1024]{1,0:T(8,128)S(1)}, u32[]{:S(2)}, u32[]{:S(2)}) collective-permute-start(f32[256,1024]{1,0:T(8,128)S(1)} %bitcast.12), channel_id=1, source_target_pairs={{0,8},{8,0},{1,9},{9,1},{2,10},{10,2},{3,11},{11,3},{4,12},{12,4},... | collective-permute-start | bytes 3145736 | tf_op jit(solution)/shard_map/ppermute | solution.py:156
  142.1 2.9 %copy-start = (f32[512,1024]{1,0:T(8,128)}, f32[512,1024]{1,0:T(8,128)S(1)}, u32[]{:S(2)}) copy-start(f32[512,1024]{1,0:T(8,128)S(1)} %get-tuple-element.18) | copy-start | bytes 6291460

commit v3 on v2

v3 whole, which is shorter than its diff:
```python
import functools

import jax
import jax.numpy as jnp
from jax import lax
from jax.experimental import pallas as pl
from jax.experimental.pallas import tpu as pltpu
from jax.sharding import Mesh, PartitionSpec as P

epsilon = 1e-06
SHARPNESS = 1.5
DP = ("x", "zl", "c")
CENT = ("zh", "y")
MASS = 128
F32, BF16 = jnp.float32, jnp.bfloat16
VMEM = 24 * 2**20
NT = (((1,), (1,)), ((), ()))
NN = (((1,), (0,)), ((), ()))


def split(value):
    high = value.astype(BF16)
    return high, (value - high.astype(F32)).astype(BF16)


def mm(left, right, dims):
    return lax.dot_general(left, right, dims, preferred_element_type=F32)


def fit_kernel(step, e_ref, c_ref, p_ref, stat_ref, eh_ref, el_ref, chl):
    @pl.when(pl.program_id(0) == 0)
    def _():
        c = c_ref[...]
        c = c * (SHARPNESS * lax.rsqrt(jnp.sum(c * c, axis=1, keepdims=True) + epsilon))
        high, low = split(c)
        for chip in range(16):
            for core in range(2):
                here, there = (chip * 2 + core) * 16, (core * 16 + chip) * 16
                chl[there : there + 16, :] = high[here : here + 16, :]
                chl[512 + there : 528 + there, :] = low[here : here + 16, :]

    for j in range(0, e_ref.shape[0], step):
        rows = slice(j, j + step)
        eh, el = split(e_ref[rows, :])
        eh_ref[rows, :] = eh
        el_ref[rows, :] = el
        k = p_ref.shape[0]
        both = mm(chl[...], eh, NT)
        logits = both[:k] + both[k:] + mm(chl[:k, :], el, NT)
        top = jnp.max(logits, axis=0, keepdims=True)
        p = jnp.exp(logits - top)
        p_ref[:, rows] = p
        stat_ref[0:1, rows] = top
        stat_ref[1:2, rows] = jnp.sum(p, axis=0, keepdims=True)


def fit(e, c, block=512, step=256):
    (n, d), k = e.shape, c.shape[0]
    return pl.pallas_call(
        functools.partial(fit_kernel, step),
        grid=(n // block,),
        in_specs=[pl.BlockSpec((block, d), lambda i: (i, 0)), pl.BlockSpec((k, d), lambda i: (0, 0))],
        out_specs=[
            pl.BlockSpec((k, block), lambda i: (0, i)),
            pl.BlockSpec((2, block), lambda i: (0, i)),
            pl.BlockSpec((block, d), lambda i: (i, 0)),
            pl.BlockSpec((block, d), lambda i: (i, 0)),
        ],
        out_shape=[
            jax.ShapeDtypeStruct((k, n), F32),
            jax.ShapeDtypeStruct((2, n), F32),
            jax.ShapeDtypeStruct((n, d), BF16),
            jax.ShapeDtypeStruct((n, d), BF16),
        ],
        scratch_shapes=[pltpu.VMEM((2 * k, d), BF16)],
        compiler_params=pltpu.CompilerParams(vmem_limit_bytes=VMEM),
        name="fit",
    )(e, c)


def sums_kernel(_, stats_ref, own_ref, eh_ref, el_ref, *refs):
    *p_refs, o_ref = refs

    @pl.when(pl.program_id(0) == 0)
    def _():
        o_ref[...] = jnp.zeros_like(o_ref)

    tops, totals = stats_ref[:, 0, :], stats_ref[:, 1, :]
    top = jnp.max(tops, axis=0, keepdims=True)
    total = jnp.sum(totals * jnp.exp(tops - top), axis=0, keepdims=True)
    scale = jnp.exp(own_ref[0:1, :] - top) / total
    w = jnp.concatenate([p_ref[...] for p_ref in p_refs], axis=0) * scale
    (k, block), d = w.shape, eh_ref.shape[1]
    here = pl.ds(pl.multiple_of(pl.program_id(0) * block, block), block)
    wh, wl = split(w)
    both = mm(jnp.concatenate([wh, wl], axis=0), eh_ref[here, :], NN)
    part = both[:k] + both[k:] + mm(wh, el_ref[here, :], NN)
    mass = jnp.broadcast_to(jnp.sum(w, axis=1, keepdims=True), (k, MASS))
    o_ref[:, :d] += part
    o_ref[:, d:] += mass


def sums(stats, own, p, eh, el, blocks, rows=64, block=1024):
    n, d = eh.shape
    count = blocks.shape[0]
    whole = pl.BlockSpec(memory_space=pltpu.VMEM)
    return pl.pallas_call(
        sums_kernel,
        grid_spec=pltpu.PrefetchScalarGridSpec(
            num_scalar_prefetch=1,
            grid=(n // block,),
            in_specs=[
                pl.BlockSpec((8, 2, block), lambda i, b: (0, 0, i)),
                pl.BlockSpec((2, block), lambda i, b: (0, i)),
                whole,
                whole,
            ]
            + [pl.BlockSpec((rows, block), lambda i, b, j=j: (b[j], i)) for j in range(count)],
            out_specs=pl.BlockSpec((rows * count, d + MASS), lambda i, b: (0, 0)),
        ),
        out_shape=jax.ShapeDtypeStruct((rows * count, d + MASS), F32),
        compiler_params=pltpu.CompilerParams(vmem_limit_bytes=VMEM),
        cost_estimate=pl.CostEstimate(flops=6 * n * d * rows * count, bytes_accessed=4 * n * d, transcendentals=0),
        name="sums",
    )(blocks, stats, own, eh, el, *[p] * count)


def prepare_kernel(c_ref, o_ref):
    c = c_ref[...]
    k = c.shape[0]
    o_ref[:k, :], o_ref[k:, :] = split(c * (SHARPNESS * lax.rsqrt(jnp.sum(c * c, axis=1, keepdims=True) + epsilon)))


def prepare(c):
    return pl.pallas_call(
        prepare_kernel,
        out_shape=jax.ShapeDtypeStruct((2 * c.shape[0], c.shape[1]), BF16),
        compiler_params=pltpu.CompilerParams(vmem_limit_bytes=VMEM),
        name="prepare",
    )(c)


def unit_rms(points):
    return points * lax.rsqrt(jnp.mean(points * points, axis=1, keepdims=True) + epsilon)


def soft_weights(high, low, centers):
    k = centers.shape[0] // 2
    logits = mm(high, centers[:k, :], NT) + mm(high, centers[k:, :], NT) + mm(low, centers[:k, :], NT)
    shifted = jnp.exp(logits - jnp.max(logits, axis=1, keepdims=True))
    return (shifted / jnp.sum(shifted, axis=1, keepdims=True)).T


def store_sums(o_ref, w, high, low):
    wh, wl = split(w)
    d = high.shape[1]
    o_ref[:, :d] = mm(wh, high, NN) + mm(wh, low, NN) + mm(wl, high, NN)
    o_ref[:, d:] = jnp.broadcast_to(jnp.sum(w, axis=1, keepdims=True), (w.shape[0], MASS))


def points_kernel(part_ref, fine_ref, spread_ref):
    part = part_ref[0] + part_ref[1] + part_ref[2] + part_ref[3]
    d = fine_ref.shape[1]
    fine = part[:, :d] / part[:, d : d + 1]
    fine_ref[...] = fine
    points = unit_rms(fine)
    for i in range(spread_ref.shape[0]):
        spread_ref[i] = points


def points_of(part, copies):
    _, n, d = part.shape
    return pl.pallas_call(
        points_kernel,
        out_shape=[
            jax.ShapeDtypeStruct((n, d - MASS), F32),
            jax.ShapeDtypeStruct((copies, n, d - MASS), F32),
        ],
        compiler_params=pltpu.CompilerParams(vmem_limit_bytes=VMEM),
        name="points",
    )(part)


def coarse_kernel(slice_ref, own_ref, other_ref, c_ref, o_ref, w_ref):
    high, low = split(jnp.concatenate([own_ref[...], other_ref[...]], axis=0))
    w_ref[...] = soft_weights(high, low, c_ref[...])
    rows = o_ref.shape[0]
    w = w_ref[pl.ds(pl.multiple_of(slice_ref[0] * rows, rows), rows), :]
    store_sums(o_ref, w, high, low)


def coarse_sums(index, own, other, centers, rows):
    n, d = own.shape
    whole = pl.BlockSpec(memory_space=pltpu.VMEM)
    return pl.pallas_call(
        coarse_kernel,
        in_specs=[pl.BlockSpec(memory_space=pltpu.SMEM), whole, whole, whole],
        out_specs=whole,
        out_shape=jax.ShapeDtypeStruct((rows, d + MASS), F32),
        scratch_shapes=[pltpu.VMEM((centers.shape[0] // 2, 2 * n), F32)],
        compiler_params=pltpu.CompilerParams(vmem_limit_bytes=VMEM),
        name="coarse",
    )(index, own, other, centers)


def top_kernel(points_ref, c_ref, o_ref):
    high, low = split(unit_rms(points_ref[...]))
    store_sums(o_ref, soft_weights(high, low, c_ref[...]), high, low)


def top_sums(points, centers):
    d = points.shape[1]
    whole = pl.BlockSpec(memory_space=pltpu.VMEM)
    return pl.pallas_call(
        top_kernel,
        in_specs=[whole, whole],
        out_specs=whole,
        out_shape=jax.ShapeDtypeStruct((centers.shape[0] // 2, d + MASS), F32),
        compiler_params=pltpu.CompilerParams(vmem_limit_bytes=VMEM),
        name="top",
    )(points, centers)


def final_kernel(core_ref, own_ref, other_ref, part_ref, add_ref, coarse_ref, top_ref, sems):
    rows = own_ref.shape[0]
    copies = []
    for i, ref in enumerate((own_ref, other_ref)):
        half = core_ref[0] if i == 0 else 1 - core_ref[0]
        there = pl.ds(pl.multiple_of(half * rows, rows), rows)
        copies.append(pltpu.make_async_copy(ref, coarse_ref.at[there, :], sems.at[i]))
        copies[i].start()
    part = part_ref[...] + add_ref[...]
    d = top_ref.shape[1]
    top_ref[...] = part[:, :d] / part[:, d : d + 1]
    for copy in copies:
        copy.wait()


def final(core, own, other, part, add):
    whole = pl.BlockSpec(memory_space=pltpu.VMEM)
    (n, d), k = own.shape, part.shape[0]
    return pl.pallas_call(
        final_kernel,
        in_specs=[pl.BlockSpec(memory_space=pltpu.SMEM)] + [whole] * 4,
        out_specs=[pl.BlockSpec(memory_space=pltpu.HBM), whole],
        out_shape=[jax.ShapeDtypeStruct((2 * n, d), F32), jax.ShapeDtypeStruct((k, d), F32)],
        scratch_shapes=[pltpu.SemaphoreType.DMA((2,))],
        compiler_params=pltpu.CompilerParams(vmem_limit_bytes=VMEM),
        name="final",
    )(core, own, other, part, add)


def spread(value, axes, size):
    return lax.all_to_all(jnp.broadcast_to(value[None], (size, *value.shape)), axes, 0, 0)


def add_up(part, axes, size):
    part = part.reshape(size, part.shape[0] // size, part.shape[1])
    return jnp.sum(lax.all_to_all(part, axes, 0, 0), axis=0)


def swap_core(value):
    return lax.ppermute(value, "c", [(0, 1), (1, 0)])


def shift(value, step):
    return lax.ppermute(value, "x", [(i, (i + step) % 4) for i in range(4)])


def body(embeddings, centroids, coarse_centroids, top_centroids):
    core = lax.axis_index("c")
    dim = embeddings.shape[1]
    embeddings, centroids = (pltpu.with_memory_space_constraint(a, pltpu.HBM) for a in (embeddings, centroids))
    p, own, eh, el = fit(embeddings, centroids)
    x = lax.axis_index("x")
    mine, theirs = 4 * core, 4 * (1 - core)
    up, down, far = (x + 1) % 4, (x + 3) % 4, (x + 2) % 4
    blocks = [
        jnp.stack(group)
        for group in (
            (theirs + far,),
            (mine + far,),
            (theirs + up, theirs + down, theirs + x),
            (mine + up, mine + down),
            (mine + x,),
        )
    ]
    own, blocks = lax.optimization_barrier((own, blocks))
    stats = spread(own, CENT, 8)
    far_in = swap_core(sums(stats, own, p, eh, el, blocks[0]))
    far_own = sums(stats, own, p, eh, el, blocks[1])
    near_in = swap_core(sums(stats, own, p, eh, el, blocks[2]))
    far_sum = far_own + far_in
    up_part, down_part = shift(far_sum[:32], 1), shift(far_sum[32:], -1)
    blocks[3], _ = lax.optimization_barrier((blocks[3], far_sum))
    near = sums(stats, own, p, eh, el, blocks[3]) + near_in[:128]
    up_sum = jnp.concatenate([near[:32] + up_part, near[32:64]], axis=0)
    down_sum = jnp.concatenate([near[64:96], near[96:] + down_part], axis=0)
    from_down, from_up = shift(up_sum, 1), shift(down_sum, -1)
    blocks[4], _ = lax.optimization_barrier((blocks[4], (up_sum, down_sum)))
    part = sums(stats, own, p, eh, el, blocks[4])
    part = part + near_in[128:] + from_down + from_up
    coarse_centroids, top_centroids, _ = lax.optimization_barrier((coarse_centroids, top_centroids, up_sum))
    coarse_centers, top_centers = prepare(coarse_centroids), prepare(top_centroids)
    fine, points = points_of(lax.all_to_all(part.reshape(4, 16, dim + MASS), "zl", 0, 0), 4)

    points = lax.all_to_all(points, "x", 0, 0).reshape(64, dim)
    part = coarse_sums((core * 4 + x).reshape(1), points, swap_core(points), coarse_centers, 64)
    part = add_up(part, ("y", "zh", "zl"), 32)
    coarse = part[:, :dim] / part[:, dim : dim + 1]
    coarse = spread(coarse, ("zh", "zl"), 8).reshape(16, dim)
    coarse = spread(coarse, ("x", "y"), 16).reshape(256, dim)
    other = swap_core(coarse)
    part = top_sums(coarse, top_centers)
    new_coarse, new_top = final(core.reshape(1), coarse, other, part, swap_core(part))
    return (fine[None], new_coarse, new_top)


def solution(mesh):
    fold = Mesh(mesh.devices.reshape(4, 4, 2, 2, 4), DP + CENT)
    in_specs = (P(DP, None), P(CENT, None), P(), P())
    out_specs = (P(CENT, DP, None), P(), P())
    return jax.shard_map(body, mesh=fold, in_specs=in_specs, out_specs=out_specs, check_vma=False)
```

time: 145 us -> 139 us (0.959)
  blocking collectives: 102 us -> 80.6 us
  Pallas kernels: 19.1 us -> 29.3 us
  starting transfers between devices: 11.3 us -> 17.6 us
  waiting for transfers between devices: 3.09 us -> 8.92 us
  matrix products: 4.38 us -> 0 us
  other arithmetic: 3.44 us -> 0.63 us
    all_to_all x3 -> x1, blocking collectives: 44.2 us -> 13.2 us  [add_up(): return jnp.sum(lax.all_to_all(part, axes, 0, 0), axis=0)]
    all_to_all x0 -> x2, blocking collectives: none -> 17.3 us  [the longest x1 9.41 us: body(): lax.all_to_all(part.reshape(4, 16, dim + MASS), 'zl', 0, 0)]
    all_to_all x4 -> x3, blocking collectives: 57.9 us -> 50 us  [spread(): lax.all_to_all(jnp.broadcast_to(value[None], (size, *value.shape)), axes,...]
    ppermute x0 -> x4, waiting for transfers between devices: none -> 6.68 us  [shift(): return lax.ppermute(value, 'x', [(i, (i + step) % 4) for i in range(4)])]
    pallas_call x0 -> x6, Pallas kernels: none -> 6.62 us  [the longest x1 2.04 us: final(): pl.pallas_call(final_kernel, in_specs=[pl.BlockSpec(memory_space=pltpu.SM...]
    ppermute x0 -> x4, starting transfers between devices: none -> 5.27 us  [shift(): return lax.ppermute(value, 'x', [(i, (i + step) % 4) for i in range(4)])]
    dot_general x4 -> x0, matrix products: 4.38 us -> none  [dot3(): lax.dot_general(left, right, (((contract_left,), (contract_right,)), ((),...]
    pallas_call x2 -> x5, Pallas kernels: 7.76 us -> 11.5 us  [sums(): pl.pallas_call(sums_kernel, grid_spec=pltpu.PrefetchScalarGridSpec(num_sc...]
  transfers between devices with their start and end apart: 3 -> 9, of which waited for: 2 -> 5; matrix products, arithmetic and copies ran while one was open for 0% -> 0% of each run, Pallas kernels for 3% -> 9%
where the time goes in v3:
time: 139 us
  blocking collectives  80.6 us (58%)
  Pallas kernels  29.3 us (21%)
  starting transfers between devices  17.6 us (13%)
  waiting for transfers between devices  8.92 us (6%)
    all_to_all x3, blocking collectives, spread(): lax.all_to_all(jnp.broadcast_to(value[None], (size, *value.shape)), axes,...  50 us
    all_to_all x1, blocking collectives, add_up(): return jnp.sum(lax.all_to_all(part, axes, 0, 0), axis=0)  13.2 us
    ppermute x5, starting transfers between devices, swap_core(): return lax.ppermute(value, 'c', [(0, 1), (1, 0)])  12.3 us
    pallas_call x5, Pallas kernels, sums(): pl.pallas_call(sums_kernel, grid_spec=pltpu.PrefetchScalarGridSpec(num_sc...  11.5 us
    pallas_call x1, Pallas kernels, fit(): pl.pallas_call(functools.partial(fit_kernel, step), grid=(n // block,), i...  11.2 us
    all_to_all x1, blocking collectives, body(): lax.all_to_all(part.reshape(4, 16, dim + MASS), 'zl', 0, 0)  9.41 us
    all_to_all x1, blocking collectives, body(): points = lax.all_to_all(points, 'x', 0, 0).reshape(64, dim)  7.9 us
    ppermute x4, waiting for transfers between devices, shift(): return lax.ppermute(value, 'x', [(i, (i + step) % 4) for i in range(4)])  6.68 us
  transfers between devices with their start and end apart: 9, of which 5 were waited for; matrix products, arithmetic and copies ran while one was open for 0% of the time, Pallas kernels for 9%

profile of v3, /device:TPU:1, one launch (start us, length us, event | category | flops | bytes accessed | tf_op | source)
XLA Modules:
  0.0 138.6 jit_solution(17481984699877666418)
XLA Ops:
  0.7 0.1 pad_add_fusion.1._
  0.7 11.2 %fit.1 = (f32[512,2048]{1,0:T(8,128)S(1)}, f32[2,2048]{1,0:T(2,128)S(1)}, bf16[2048,1024]{1,0:T(8,128)(2,1)S(1)}, bf16[2048,1024]{1,0:T(8,128)(2,1)S(1)}) custom-call(f32[2048,1024]{1,0:T(8,128)} %e_ref.1, f32[512,1024]{1,0:T(8,128)} %c_ref.1), custom_call_target="tpu_custom_call" | custom-call | tf_op jit(solution)/shard_map/fit/pallas_call | solution.py:59
  11.9 0.1 pad_add_fusion._
  12.1 20.8 %all_to_all.30.stats_ref = f32[8,2,2048]{2,1,0:T(2,128)S(1)} all-to-all(f32[8,2,2048]{2,1,0:T(2,128)S(1)} %broadcast_in_dim.10), channel_id=1, replica_groups=mesh['x'=4,'zl'=4,'c'=2,'zh'=2,'y'=4] {'zh','y'}, dimensions={0} | all-to-all | bytes 262144 | tf_op jit(solution)/shard_map/all_to_all | solution.py:254
  32.9 1.7 %sums.6 = f32[64,1152]{1,0:T(8,128)S(1)} custom-call(s32[1]{0:T(128)} %bitcast._, f32[8,2,2048]{2,1,0:T(2,128)S(1)} %all_to_all.30.stats_ref, f32[2,2048]{1,0:T(2,128)S(1)} %get-tuple-element.25.own_ref, bf16[2048,1024]{1,0:T(8,128)(2,1)S(1)} %get-tuple-element.26.eh_ref, bf16[2048,1024]{1,0:T(8,128)(2,1)S(1)} %get-tuple-element.27.el_ref, ...), custom_call_target="tpu_custom_call" | custom-call | flops 805306368 | bytes 8388608 | tf_op jit(solution)/shard_map/sums/pallas_call | solution.py:107
  34.6 2.2 %collective-permute-start = (f32[64,1152]{1,0:T(8,128)S(1)}, f32[64,1152]{1,0:T(8,128)S(1)}, u32[]{:S(2)}, u32[]{:S(2)}) collective-permute-start(f32[64,1152]{1,0:T(8,128)S(1)} %sums.6), channel_id=1, source_target_pairs={{0,8},{8,0},{1,9},{9,1},{2,10},{10,2},{3,11},{11,3},{4,12},{12,4},... | collective-permute-start | bytes 884744 | tf_op jit(solution)/shard_map/ppermute | solution.py:263
  36.8 3.6 %sums.8 = f32[192,1152]{1,0:T(8,128)S(1)} custom-call(s32[3]{0:T(128)S(1)} %pad_add_fusion._, f32[8,2,2048]{2,1,0:T(2,128)S(1)} %all_to_all.30.stats_ref, f32[2,2048]{1,0:T(2,128)S(1)} %get-tuple-element.25.own_ref, bf16[2048,1024]{1,0:T(8,128)(2,1)S(1)} %get-tuple-element.26.eh_ref, bf16[2048,1024]{1,0:T(8,128)(2,1)S(1)} %get-tuple-element.27.el_ref, ...), custom_call_target="tpu_custom_call" | custom-call | flops 2415919104 | bytes 8388608 | tf_op jit(solution)/shard_map/sums/pallas_call | solution.py:107
  40.4 0.1 collective-permute-start.1
  40.5 1.7 %sums.5 = f32[64,1152]{1,0:T(8,128)S(1)} custom-call(s32[1]{0:T(128)} %bitcast.1._, f32[8,2,2048]{2,1,0:T(2,128)S(1)} %all_to_all.30.stats_ref, f32[2,2048]{1,0:T(2,128)S(1)} %get-tuple-element.25.own_ref, bf16[2048,1024]{1,0:T(8,128)(2,1)S(1)} %get-tuple-element.26.eh_ref, bf16[2048,1024]{1,0:T(8,128)(2,1)S(1)} %get-tuple-element.27.el_ref, ...), custom_call_target="tpu_custom_call" | custom-call | flops 805306368 | bytes 8388608 | tf_op jit(solution)/shard_map/sums/pallas_call | solution.py:107
  42.2 0.0 collective-permute-done
  42.3 1.3 collective-permute-start.2
  43.6 1.5 %collective-permute-start.3 = (f32[32,1152]{1,0:T(8,128)S(1)}, f32[32,1152]{1,0:T(8,128)S(1)}, u32[]{:S(2)}, u32[]{:S(2)}) collective-permute-start(f32[32,1152]{1,0:T(8,128)S(1)} %get-tuple-element.44), channel_id=1, source_target_pairs={{0,192},{64,0},{128,64},{192,128},{1,193},{65,1},{129,65},{193,129... | collective-permute-start | bytes 442376 | tf_op jit(solution)/shard_map/ppermute | solution.py:267
  45.1 2.8 %sums.7 = f32[128,1152]{1,0:T(8,128)S(1)} custom-call(s32[2]{0:T(128)S(1)} %pad_add_fusion.1._, f32[8,2,2048]{2,1,0:T(2,128)S(1)} %all_to_all.30.stats_ref, f32[2,2048]{1,0:T(2,128)S(1)} %get-tuple-element.25.own_ref, bf16[2048,1024]{1,0:T(8,128)(2,1)S(1)} %get-tuple-element.26.eh_ref, bf16[2048,1024]{1,0:T(8,128)(2,1)S(1)} %get-tuple-element.27.el_ref, ...), custom_call_target="tpu_custom_call" | custom-call | flops 1610612736 | bytes 8388608 | tf_op jit(solution)/shard_map/sums/pallas_call | solution.py:107
  47.8 0.0 collective-permute-done.1
  47.8 0.1 slice_add_fusion
  47.9 0.6 collective-permute-done.2
  48.5 0.0 collective-permute-done.3
  48.5 0.1 slice_add_fusion.3
  48.6 2.4 %collective-permute-start.5 = (f32[64,1152]{1,0:T(8,128)S(1)}, f32[64,1152]{1,0:T(8,128)S(1)}, u32[]{:S(2)}, u32[]{:S(2)}) collective-permute-start(f32[64,1152]{1,0:T(8,128)S(1)} %pad_maximum_fusion.1), channel_id=1, source_target_pairs={{0,192},{64,0},{128,64},{192,128},{1,193},{65,1},{129,65},{193,129... | collective-permute-start | bytes 884744 | tf_op jit(solution)/shard_map/ppermute | solution.py:267
  51.1 0.1 collective-permute-start.4
  51.2 1.7 %sums.9 = f32[64,1152]{1,0:T(8,128)S(1)} custom-call(s32[1]{0:T(128)} %bitcast.7._.slice_ref, f32[8,2,2048]{2,1,0:T(2,128)S(1)} %all_to_all.30.stats_ref, f32[2,2048]{1,0:T(2,128)S(1)} %get-tuple-element.25.own_ref, bf16[2048,1024]{1,0:T(8,128)(2,1)S(1)} %get-tuple-element.26.eh_ref, bf16[2048,1024]{1,0:T(8,128)(2,1)S(1)} %get-tuple-element.27.el_ref, ...), custom_call_target="tpu_custom_call" | custom-call | flops 805306368 | bytes 8388608 | tf_op jit(solution)/shard_map/sums/pallas_call | solution.py:107
  52.9 0.0 copy-start
  52.9 3.0 %collective-permute-done.5 = f32[64,1152]{1,0:T(8,128)S(1)} collective-permute-done((f32[64,1152]{1,0:T(8,128)S(1)}, f32[64,1152]{1,0:T(8,128)S(1)}, u32[]{:S(2)}, u32[]{:S(2)}) %collective-permute-start.5) | collective-permute-done | bytes 294944 | tf_op jit(solution)/shard_map/ppermute | solution.py:267
  55.9 3.1 %collective-permute-done.4 = f32[64,1152]{1,0:T(8,128)S(1)} collective-permute-done((f32[64,1152]{1,0:T(8,128)S(1)}, f32[64,1152]{1,0:T(8,128)S(1)}, u32[]{:S(2)}, u32[]{:S(2)}) %collective-permute-start.4) | collective-permute-done | bytes 294944 | tf_op jit(solution)/shard_map/ppermute | solution.py:267
  59.0 0.1 fusion.1
  59.0 9.4 %all_to_all.31.part_ref = f32[4,16,1152]{2,1,0:T(8,128)S(1)} all-to-all(f32[4,16,1152]{2,1,0:T(8,128)S(1)} %bitcast.18), channel_id=1, replica_groups=mesh['x'=4,'zl'=4,'c'=2,'zh'=2,'y'=4] {'zl'}, dimensions={0} | all-to-all | bytes 589824 | tf_op jit(solution)/shard_map/all_to_all | solution.py:305
  68.5 0.7 points.1
  69.2 7.9 %all_to_all.32 = f32[4,16,1024]{2,1,0:T(8,128)S(1)} all-to-all(f32[4,16,1024]{2,1,0:T(8,128)S(1)} %get-tuple-element.34), channel_id=1, replica_groups=mesh['x'=4,'zl'=4,'c'=2,'zh'=2,'y'=4] {'x'}, dimensions={0} | all-to-all | bytes 524288 | tf_op jit(solution)/shard_map/all_to_all | solution.py:307
  77.1 5.3 %collective-permute-start.6 = (f32[64,1024]{1,0:T(8,128)S(1)}, f32[64,1024]{1,0:T(8,128)S(1)}, u32[]{:S(2)}, u32[]{:S(2)}) collective-permute-start(f32[64,1024]{1,0:T(8,128)S(1)} %bitcast.16), channel_id=1, source_target_pairs={{0,8},{8,0},{1,9},{9,1},{2,10},{10,2},{3,11},{11,3},{4,12},{12,4},... | collective-permute-start | bytes 786440 | tf_op jit(solution)/shard_map/ppermute | solution.py:263
  82.4 0.5 prepare.2.c_ref
  82.9 0.0 copy-start.1
  82.9 0.7 collective-permute-done.6.other_ref
  83.5 1.7 %coarse.1 = f32[64,1152]{1,0:T(8,128)S(1)} custom-call(s32[1]{0:T(128)} %bitcast.7._.slice_ref, f32[64,1024]{1,0:T(8,128)S(1)} %bitcast.17, f32[64,1024]{1,0:T(8,128)S(1)} %collective-permute-done.6.other_ref, bf16[1024,1024]{1,0:T(8,128)(2,1)S(1)} %prepare.2.c_ref), custom_call_target="tpu_custom_call" | custom-call | tf_op jit(solution)/shard_map/coarse/pallas_call | solution.py:195
  85.2 0.2 reshape.28
  85.4 13.2 %all_to_all.33 = f32[32,2,1152]{2,1,0:T(2,128)S(1)} all-to-all(f32[32,2,1152]{2,1,0:T(2,128)S(1)} %reshape.28), channel_id=1, replica_groups=mesh['x'=4,'zl'=4,'c'=2,'zh'=2,'y'=4] {'y','zh','zl'}, dimensions={0} | all-to-all | bytes 589824 | tf_op jit(solution)/shard_map/all_to_all | solution.py:259
  98.6 0.1 reduce_sum.9
  98.7 0.1 slice_reduce_fusion
  98.8 0.1 slice_divide_fusion
  99.0 12.0 %all_to_all.34 = f32[8,2,1024]{2,1,0:T(2,128)S(1)} all-to-all(f32[8,2,1024]{2,1,0:T(2,128)S(1)} %broadcast_in_dim.24), channel_id=1, replica_groups=mesh['x'=4,'zl'=4,'c'=2,'zh'=2,'y'=4] {'zh','zl'}, dimensions={0} | all-to-all | bytes 131072 | tf_op jit(solution)/shard_map/all_to_all | solution.py:254
  111.0 0.1 broadcast_in_dim.26
  111.1 17.2 %all_to_all.35 = f32[16,16,1024]{2,1,0:T(8,128)S(1)} all-to-all(f32[16,16,1024]{2,1,0:T(8,128)S(1)} %broadcast_in_dim.26), channel_id=1, replica_groups=mesh['x'=4,'zl'=4,'c'=2,'zh'=2,'y'=4] {'x','y'}, dimensions={0} | all-to-all | bytes 2097152 | tf_op jit(solution)/shard_map/all_to_all | solution.py:254
  128.4 4.6 %collective-permute-start.7 = (f32[256,1024]{1,0:T(8,128)S(1)}, f32[256,1024]{1,0:T(8,128)S(1)}, u32[]{:S(2)}, u32[]{:S(2)}) collective-permute-start(f32[256,1024]{1,0:T(8,128)S(1)} %bitcast.13), channel_id=1, source_target_pairs={{0,8},{8,0},{1,9},{9,1},{2,10},{10,2},{3,11},{11,3},{4,12},{12,4},... | collective-permute-start | bytes 3145736 | tf_op jit(solution)/shard_map/ppermute | solution.py:263
  133.0 0.1 prepare.3.c_ref
  133.1 1.6 %top.1.part_ref = f32[64,1152]{1,0:T(8,128)S(1)} custom-call(f32[256,1024]{1,0:T(8,128)S(1)} %bitcast.14, bf16[128,1024]{1,0:T(8,128)(2,1)S(1)} %prepare.3.c_ref), custom_call_target="tpu_custom_call" | custom-call | tf_op jit(solution)/shard_map/top/pallas_call | solution.py:214
  134.7 0.1 collective-permute-start.8
  134.8 1.6 %collective-permute-done.8.add_ref = f32[64,1152]{1,0:T(8,128)S(1)} collective-permute-done((f32[64,1152]{1,0:T(8,128)S(1)}, f32[64,1152]{1,0:T(8,128)S(1)}, u32[]{:S(2)}, u32[]{:S(2)}) %collective-permute-start.8) | collective-permute-done | bytes 294944 | tf_op jit(solution)/shard_map/ppermute | solution.py:263
  136.4 0.0 collective-permute-done.7.other_ref
  136.4 2.0 %final.1 = (f32[512,1024]{1,0:T(8,128)}, f32[64,1024]{1,0:T(8,128)}) custom-call(s32[1]{0:T(128)} %bitcast.10.core_ref, f32[256,1024]{1,0:T(8,128)S(1)} %bitcast.15, f32[256,1024]{1,0:T(8,128)S(1)} %collective-permute-done.7.other_ref, f32[64,1152]{1,0:T(8,128)S(1)} %top.1.part_ref, f32[64,1152]{1,0:T(8,128)S(1)} %collective-permute-done.8.add_ref), custom_call_target="tpu_custom_call" | custom-call | tf_op jit(solution)/shard_map/final/pallas_call | solution.py:242
  (9 shorter events, 0.2 us)
Async XLA Ops:
  34.6 7.7 %collective-permute-start = (f32[64,1152]{1,0:T(8,128)S(1)}, f32[64,1152]{1,0:T(8,128)S(1)}, u32[]{:S(2)}, u32[]{:S(2)}) collective-permute-start(f32[64,1152]{1,0:T(8,128)S(1)} %sums.6), channel_id=1, source_target_pairs={{0,8},{8,0},{1,9},{9,1},{2,10},{10,2},{3,11},{11,3},{4,12},{12,4},... | collective-permute-start | bytes 884744 | tf_op jit(solution)/shard_map/ppermute | solution.py:263
  40.4 7.4 %collective-permute-start.1 = (f32[192,1152]{1,0:T(8,128)S(1)}, f32[192,1152]{1,0:T(8,128)S(1)}, u32[]{:S(2)}, u32[]{:S(2)}) collective-permute-start(f32[192,1152]{1,0:T(8,128)S(1)} %sums.8), channel_id=1, source_target_pairs={{0,8},{8,0},{1,9},{9,1},{2,10},{10,2},{3,11},{11,3},{4,12},{12,4},... | collective-permute-start | bytes 2654216 | tf_op jit(solution)/shard_map/ppermute | solution.py:263
  42.3 6.2 %collective-permute-start.2 = (f32[32,1152]{1,0:T(8,128)S(1)}, f32[32,1152]{1,0:T(8,128)S(1)}, u32[]{:S(2)}, u32[]{:S(2)}) collective-permute-start(f32[32,1152]{1,0:T(8,128)S(1)} %get-tuple-element.43), channel_id=1, source_target_pairs={{0,64},{64,128},{128,192},{192,0},{1,65},{65,129},{129,193},{193,1... | collective-permute-start | bytes 442376 | tf_op jit(solution)/shard_map/ppermute | solution.py:267
  43.6 5.0 %collective-permute-start.3 = (f32[32,1152]{1,0:T(8,128)S(1)}, f32[32,1152]{1,0:T(8,128)S(1)}, u32[]{:S(2)}, u32[]{:S(2)}) collective-permute-start(f32[32,1152]{1,0:T(8,128)S(1)} %get-tuple-element.44), channel_id=1, source_target_pairs={{0,192},{64,0},{128,64},{192,128},{1,193},{65,1},{129,65},{193,129... | collective-permute-start | bytes 442376 | tf_op jit(solution)/shard_map/ppermute | solution.py:267
  48.6 7.3 %collective-permute-start.5 = (f32[64,1152]{1,0:T(8,128)S(1)}, f32[64,1152]{1,0:T(8,128)S(1)}, u32[]{:S(2)}, u32[]{:S(2)}) collective-permute-start(f32[64,1152]{1,0:T(8,128)S(1)} %pad_maximum_fusion.1), channel_id=1, source_target_pairs={{0,192},{64,0},{128,64},{192,128},{1,193},{65,1},{129,65},{193,129... | collective-permute-start | bytes 884744 | tf_op jit(solution)/shard_map/ppermute | solution.py:267
  51.1 7.9 %collective-permute-start.4 = (f32[64,1152]{1,0:T(8,128)S(1)}, f32[64,1152]{1,0:T(8,128)S(1)}, u32[]{:S(2)}, u32[]{:S(2)}) collective-permute-start(f32[64,1152]{1,0:T(8,128)S(1)} %pad_maximum_fusion), channel_id=1, source_target_pairs={{0,64},{64,128},{128,192},{192,0},{1,65},{65,129},{129,193},{193,1... | collective-permute-start | bytes 884744 | tf_op jit(solution)/shard_map/ppermute | solution.py:267
  52.9 29.5 %copy-start = (f32[512,1024]{1,0:T(8,128)S(1)}, f32[512,1024]{1,0:T(8,128)}, u32[]{:S(2)}) copy-start(f32[512,1024]{1,0:T(8,128)} %c_ref.2) | copy-start | bytes 6291460
  77.1 6.5 %collective-permute-start.6 = (f32[64,1024]{1,0:T(8,128)S(1)}, f32[64,1024]{1,0:T(8,128)S(1)}, u32[]{:S(2)}, u32[]{:S(2)}) collective-permute-start(f32[64,1024]{1,0:T(8,128)S(1)} %bitcast.16), channel_id=1, source_target_pairs={{0,8},{8,0},{1,9},{9,1},{2,10},{10,2},{3,11},{11,3},{4,12},{12,4},... | collective-permute-start | bytes 786440 | tf_op jit(solution)/shard_map/ppermute | solution.py:263
  82.9 50.1 %copy-start.1 = (f32[64,1024]{1,0:T(8,128)S(1)}, f32[64,1024]{1,0:T(8,128)}, u32[]{:S(2)}) copy-start(f32[64,1024]{1,0:T(8,128)} %c_ref.3) | copy-start | bytes 786436
  128.4 8.0 %collective-permute-start.7 = (f32[256,1024]{1,0:T(8,128)S(1)}, f32[256,1024]{1,0:T(8,128)S(1)}, u32[]{:S(2)}, u32[]{:S(2)}) collective-permute-start(f32[256,1024]{1,0:T(8,128)S(1)} %bitcast.13), channel_id=1, source_target_pairs={{0,8},{8,0},{1,9},{9,1},{2,10},{10,2},{3,11},{11,3},{4,12},{12,4},... | collective-permute-start | bytes 3145736 | tf_op jit(solution)/shard_map/ppermute | solution.py:263
  134.7 1.7 %collective-permute-start.8 = (f32[64,1152]{1,0:T(8,128)S(1)}, f32[64,1152]{1,0:T(8,128)S(1)}, u32[]{:S(2)}, u32[]{:S(2)}) collective-permute-start(f32[64,1152]{1,0:T(8,128)S(1)} %top.1.part_ref), channel_id=1, source_target_pairs={{0,8},{8,0},{1,9},{9,1},{2,10},{10,2},{3,11},{11,3},{4,12},{12,4},... | collective-permute-start | bytes 884744 | tf_op jit(solution)/shard_map/ppermute | solution.py:263

commit v4 on v3

--- a/solution.py
+++ b/solution.py
@@ -13,7 +13,7 @@
 CENT = ("zh", "y")
 MASS = 128
 F32, BF16 = jnp.float32, jnp.bfloat16
-VMEM = 24 * 2**20
+VMEM = 36 * 2**20
 NT = (((1,), (1,)), ((), ()))
 NN = (((1,), (0,)), ((), ()))
 
@@ -27,24 +27,34 @@
     return lax.dot_general(left, right, dims, preferred_element_type=F32)
 
 
-def fit_kernel(step, e_ref, c_ref, p_ref, stat_ref, eh_ref, el_ref, chl):
-    @pl.when(pl.program_id(0) == 0)
-    def _():
-        c = c_ref[...]
-        c = c * (SHARPNESS * lax.rsqrt(jnp.sum(c * c, axis=1, keepdims=True) + epsilon))
-        high, low = split(c)
-        for chip in range(16):
-            for core in range(2):
-                here, there = (chip * 2 + core) * 16, (core * 16 + chip) * 16
-                chl[there : there + 16, :] = high[here : here + 16, :]
-                chl[512 + there : 528 + there, :] = low[here : here + 16, :]
-
-    for j in range(0, e_ref.shape[0], step):
-        rows = slice(j, j + step)
+def fit_kernel(step, e_hbm, c_hbm, p_ref, stat_ref, eh_ref, el_ref, chl, c_ref, e_ref, sems):
+    (n, _), k = e_ref.shape, c_ref.shape[0]
+    pieces = 4
+    copies = []
+    for i in range(pieces):
+        rows = pl.ds(i * (k // pieces), k // pieces)
+        copies.append(pltpu.make_async_copy(c_hbm.at[rows, :], c_ref.at[rows, :], sems.at[n // step + i]))
+    for i in range(n // step):
+        rows = pl.ds(i * step, step)
+        copies.append(pltpu.make_async_copy(e_hbm.at[rows, :], e_ref.at[rows, :], sems.at[i]))
+    for copy in copies:
+        copy.start()
+    for chip in range(16):
+        if chip % (16 // pieces) == 0:
+            copies[chip // (16 // pieces)].wait()
+        for core in range(2):
+            here, there = (chip * 2 + core) * 16, (core * 16 + chip) * 16
+            c = c_ref[here : here + 16, :]
+            c = c * (SHARPNESS * lax.rsqrt(jnp.sum(c * c, axis=1, keepdims=True) + epsilon))
+            chl[there : there + 16, :], chl[k + there : k + there + 16, :] = split(c)
+
+    @pl.loop(0, n // step)
+    def _(i):
+        rows = pl.ds(pl.multiple_of(i * step, step), step)
+        pltpu.make_async_copy(e_hbm.at[rows, :], e_ref.at[rows, :], sems.at[i]).wait()
         eh, el = split(e_ref[rows, :])
         eh_ref[rows, :] = eh
         el_ref[rows, :] = el
-        k = p_ref.shape[0]
         both = mm(chl[...], eh, NT)
         logits = both[:k] + both[k:] + mm(chl[:k, :], el, NT)
         top = jnp.max(logits, axis=0, keepdims=True)
@@ -54,25 +64,24 @@
         stat_ref[1:2, rows] = jnp.sum(p, axis=0, keepdims=True)
 
 
-def fit(e, c, block=512, step=256):
+def fit(e, c, step=512):
     (n, d), k = e.shape, c.shape[0]
     return pl.pallas_call(
         functools.partial(fit_kernel, step),
-        grid=(n // block,),
-        in_specs=[pl.BlockSpec((block, d), lambda i: (i, 0)), pl.BlockSpec((k, d), lambda i: (0, 0))],
-        out_specs=[
-            pl.BlockSpec((k, block), lambda i: (0, i)),
-            pl.BlockSpec((2, block), lambda i: (0, i)),
-            pl.BlockSpec((block, d), lambda i: (i, 0)),
-            pl.BlockSpec((block, d), lambda i: (i, 0)),
-        ],
+        in_specs=[pl.BlockSpec(memory_space=pltpu.HBM)] * 2,
+        out_specs=[pl.BlockSpec(memory_space=pltpu.VMEM)] * 4,
         out_shape=[
             jax.ShapeDtypeStruct((k, n), F32),
             jax.ShapeDtypeStruct((2, n), F32),
             jax.ShapeDtypeStruct((n, d), BF16),
             jax.ShapeDtypeStruct((n, d), BF16),
         ],
-        scratch_shapes=[pltpu.VMEM((2 * k, d), BF16)],
+        scratch_shapes=[
+            pltpu.VMEM((2 * k, d), BF16),
+            pltpu.VMEM((k, d), F32),
+            pltpu.VMEM((n, d), F32),
+            pltpu.SemaphoreType.DMA((n // step + 4,)),
+        ],
         compiler_params=pltpu.CompilerParams(vmem_limit_bytes=VMEM),
         name="fit",
     )(e, c)
@@ -158,24 +167,19 @@
     o_ref[:, d:] = jnp.broadcast_to(jnp.sum(w, axis=1, keepdims=True), (w.shape[0], MASS))
 
 
-def points_kernel(part_ref, fine_ref, spread_ref):
+def points_kernel(part_ref, fine_ref, points_ref):
     part = part_ref[0] + part_ref[1] + part_ref[2] + part_ref[3]
     d = fine_ref.shape[1]
     fine = part[:, :d] / part[:, d : d + 1]
     fine_ref[...] = fine
-    points = unit_rms(fine)
-    for i in range(spread_ref.shape[0]):
-        spread_ref[i] = points
-
-
-def points_of(part, copies):
+    points_ref[...] = unit_rms(fine)
+
+
+def points_of(part):
     _, n, d = part.shape
     return pl.pallas_call(
         points_kernel,
-        out_shape=[
-            jax.ShapeDtypeStruct((n, d - MASS), F32),
-            jax.ShapeDtypeStruct((copies, n, d - MASS), F32),
-        ],
+        out_shape=[jax.ShapeDtypeStruct((n, d - MASS), F32)] * 2,
         compiler_params=pltpu.CompilerParams(vmem_limit_bytes=VMEM),
         name="points",
     )(part)
@@ -203,51 +207,61 @@
     )(index, own, other, centers)
 
 
-def top_kernel(points_ref, c_ref, o_ref):
-    high, low = split(unit_rms(points_ref[...]))
+def half_copy(core, ref, coarse_ref, sem):
+    rows = ref.shape[0]
+    there = pl.ds(pl.multiple_of(core * rows, rows), rows)
+    return pltpu.make_async_copy(ref, coarse_ref.at[there, :], sem)
+
+
+def top_kernel(core_ref, own_ref, c_ref, o_ref, coarse_ref, sem):
+    copy = half_copy(core_ref[0], own_ref, coarse_ref, sem)
+    copy.start()
+    high, low = split(unit_rms(own_ref[...]))
     store_sums(o_ref, soft_weights(high, low, c_ref[...]), high, low)
-
-
-def top_sums(points, centers):
-    d = points.shape[1]
+    copy.wait()
+
+
+def top_sums(core, own, centers):
+    n, d = own.shape
     whole = pl.BlockSpec(memory_space=pltpu.VMEM)
     return pl.pallas_call(
         top_kernel,
-        in_specs=[whole, whole],
-        out_specs=whole,
-        out_shape=jax.ShapeDtypeStruct((centers.shape[0] // 2, d + MASS), F32),
+        in_specs=[pl.BlockSpec(memory_space=pltpu.SMEM), whole, whole],
+        out_specs=[whole, pl.BlockSpec(memory_space=pltpu.HBM)],
+        out_shape=[
+            jax.ShapeDtypeStruct((centers.shape[0] // 2, d + MASS), F32),
+            jax.ShapeDtypeStruct((2 * n, d), F32),
+        ],
+        scratch_shapes=[pltpu.SemaphoreType.DMA],
         compiler_params=pltpu.CompilerParams(vmem_limit_bytes=VMEM),
         name="top",
-    )(points, centers)
-
-
-def final_kernel(core_ref, own_ref, other_ref, part_ref, add_ref, coarse_ref, top_ref, sems):
-    rows = own_ref.shape[0]
-    copies = []
-    for i, ref in enumerate((own_ref, other_ref)):
-        half = core_ref[0] if i == 0 else 1 - core_ref[0]
-        there = pl.ds(pl.multiple_of(half * rows, rows), rows)
-        copies.append(pltpu.make_async_copy(ref, coarse_ref.at[there, :], sems.at[i]))
-        copies[i].start()
+    )(core, own, centers)
+
+
+def final_kernel(core_ref, _, other_ref, part_ref, add_ref, coarse_ref, top_ref, sem):
+    copy = half_copy(1 - core_ref[0], other_ref, coarse_ref, sem)
+    copy.start()
     part = part_ref[...] + add_ref[...]
     d = top_ref.shape[1]
     top_ref[...] = part[:, :d] / part[:, d : d + 1]
-    for copy in copies:
-        copy.wait()
-
-
-def final(core, own, other, part, add):
-    whole = pl.BlockSpec(memory_space=pltpu.VMEM)
-    (n, d), k = own.shape, part.shape[0]
+    copy.wait()
+
+
+def final(core, coarse, other, part, add):
+    whole, hbm = pl.BlockSpec(memory_space=pltpu.VMEM), pl.BlockSpec(memory_space=pltpu.HBM)
     return pl.pallas_call(
         final_kernel,
-        in_specs=[pl.BlockSpec(memory_space=pltpu.SMEM)] + [whole] * 4,
-        out_specs=[pl.BlockSpec(memory_space=pltpu.HBM), whole],
-        out_shape=[jax.ShapeDtypeStruct((2 * n, d), F32), jax.ShapeDtypeStruct((k, d), F32)],
-        scratch_shapes=[pltpu.SemaphoreType.DMA((2,))],
+        in_specs=[pl.BlockSpec(memory_space=pltpu.SMEM), hbm, whole, whole, whole],
+        out_specs=[hbm, whole],
+        out_shape=[
+            jax.ShapeDtypeStruct(coarse.shape, F32),
+            jax.ShapeDtypeStruct((part.shape[0], coarse.shape[1]), F32),
+        ],
+        scratch_shapes=[pltpu.SemaphoreType.DMA],
+        input_output_aliases={1: 0},
         compiler_params=pltpu.CompilerParams(vmem_limit_bytes=VMEM),
         name="final",
-    )(core, own, other, part, add)
+    )(core, coarse, other, part, add)
 
 
 def spread(value, axes, size):
@@ -265,6 +279,13 @@
 
 def shift(value, step):
     return lax.ppermute(value, "x", [(i, (i + step) % 4) for i in range(4)])
+
+
+def trade(values, axis):
+    return [
+        lax.ppermute(value, axis, [(i, i ^ flip) for i in range(4)])
+        for value, flip in zip(values, (1, 3, 2), strict=True)
+    ]
 
 
 def body(embeddings, centroids, coarse_centroids, top_centroids):
@@ -302,17 +323,18 @@
     part = part + near_in[128:] + from_down + from_up
     coarse_centroids, top_centroids, _ = lax.optimization_barrier((coarse_centroids, top_centroids, up_sum))
     coarse_centers, top_centers = prepare(coarse_centroids), prepare(top_centroids)
-    fine, points = points_of(lax.all_to_all(part.reshape(4, 16, dim + MASS), "zl", 0, 0), 4)
-
-    points = lax.all_to_all(points, "x", 0, 0).reshape(64, dim)
+    part, coarse_centers, top_centers = lax.optimization_barrier((part, coarse_centers, top_centers))
+    fine, points = points_of(lax.all_to_all(part.reshape(4, 16, dim + MASS), "zl", 0, 0))
+
+    points = jnp.concatenate([points, *trade([points] * 3, "x")], axis=0)
     part = coarse_sums((core * 4 + x).reshape(1), points, swap_core(points), coarse_centers, 64)
     part = add_up(part, ("y", "zh", "zl"), 32)
     coarse = part[:, :dim] / part[:, dim : dim + 1]
     coarse = spread(coarse, ("zh", "zl"), 8).reshape(16, dim)
     coarse = spread(coarse, ("x", "y"), 16).reshape(256, dim)
     other = swap_core(coarse)
-    part = top_sums(coarse, top_centers)
-    new_coarse, new_top = final(core.reshape(1), coarse, other, part, swap_core(part))
+    part, new_coarse = top_sums(core.reshape(1), coarse, top_centers)
+    new_coarse, new_top = final(core.reshape(1), new_coarse, other, part, swap_core(part))
     return (fine[None], new_coarse, new_top)
 
 

time: 139 us -> 136 us (0.978)
  blocking collectives: 80.6 us -> 73.2 us
  starting transfers between devices: 17.6 us -> 20.3 us
  waiting for transfers between devices: 8.92 us -> 11 us
    all_to_all x1 -> x0, blocking collectives: 7.9 us -> none  [body(): points = lax.all_to_all(points, 'x', 0, 0).reshape(64, dim)]
    ppermute x0 -> x3, starting transfers between devices: none -> 2.65 us  [trade(): lax.ppermute(value, axis, [(i, i ^ flip) for i in range(4)])]
    ppermute x0 -> x3, waiting for transfers between devices: none -> 2.37 us  [trade(): lax.ppermute(value, axis, [(i, i ^ flip) for i in range(4)])]
  transfers between devices with their start and end apart: 9 -> 12, of which waited for: 5 -> 7; matrix products, arithmetic and copies ran while one was open for 0% -> 0% of each run, Pallas kernels for 9% -> 9%
where the time goes in v4:
time: 136 us; the launch traced here: 135 us
  blocking collectives  73.2 us (54%)
  Pallas kernels  28.6 us (21%)
  starting transfers between devices  20.3 us (15%)
  waiting for transfers between devices  11 us (8%)
    all_to_all x3, blocking collectives, spread(): lax.all_to_all(jnp.broadcast_to(value[None], (size, *value.shape)), axes,...  50.5 us
    all_to_all x1, blocking collectives, add_up(): return jnp.sum(lax.all_to_all(part, axes, 0, 0), axis=0)  13.3 us
    ppermute x5, starting transfers between devices, swap_core(): return lax.ppermute(value, 'c', [(0, 1), (1, 0)])  12.4 us
    pallas_call x5, Pallas kernels, sums(): pl.pallas_call(sums_kernel, grid_spec=pltpu.PrefetchScalarGridSpec(num_sc...  11.7 us
    pallas_call x1, Pallas kernels, fit(): pl.pallas_call(functools.partial(fit_kernel, step), in_specs=[pl.BlockSpe...  10.6 us
    all_to_all x1, blocking collectives, body(): lax.all_to_all(part.reshape(4, 16, dim + MASS), 'zl', 0, 0)  9.44 us
    ppermute x4, waiting for transfers between devices, shift(): return lax.ppermute(value, 'x', [(i, (i + step) % 4) for i in range(4)])  5.94 us
    ppermute x4, starting transfers between devices, shift(): return lax.ppermute(value, 'x', [(i, (i + step) % 4) for i in range(4)])  5.27 us
  transfers between devices with their start and end apart: 12, of which 7 were waited for; matrix products, arithmetic and copies ran while one was open for 0% of the time, Pallas kernels for 9%

profile of v4, /device:TPU:1, one launch (start us, length us, event | category | flops | bytes accessed | tf_op | source)
XLA Modules:
  0.0 135.4 jit_solution(17864599938377619293)
XLA Ops:
  0.7 0.1 pad_add_fusion.1._
  0.7 10.6 %fit.1 = (f32[512,2048]{1,0:T(8,128)S(1)}, f32[2,2048]{1,0:T(2,128)S(1)}, bf16[2048,1024]{1,0:T(8,128)(2,1)S(1)}, bf16[2048,1024]{1,0:T(8,128)(2,1)S(1)}) custom-call(f32[2048,1024]{1,0:T(8,128)} %e_hbm.1, f32[512,1024]{1,0:T(8,128)} %c_hbm.1), custom_call_target="tpu_custom_call" | custom-call | tf_op jit(solution)/shard_map/fit/pallas_call | solution.py:69
  11.4 0.1 pad_add_fusion._
  11.5 20.8 %all_to_all.25.stats_ref = f32[8,2,2048]{2,1,0:T(2,128)S(1)} all-to-all(f32[8,2,2048]{2,1,0:T(2,128)S(1)} %broadcast_in_dim.10), channel_id=1, replica_groups=mesh['x'=4,'zl'=4,'c'=2,'zh'=2,'y'=4] {'zh','y'}, dimensions={0} | all-to-all | bytes 262144 | tf_op jit(solution)/shard_map/all_to_all | solution.py:268
  32.3 1.7 %sums.6 = f32[64,1152]{1,0:T(8,128)S(1)} custom-call(s32[1]{0:T(128)} %bitcast._, f32[8,2,2048]{2,1,0:T(2,128)S(1)} %all_to_all.25.stats_ref, f32[2,2048]{1,0:T(2,128)S(1)} %get-tuple-element.30.own_ref, bf16[2048,1024]{1,0:T(8,128)(2,1)S(1)} %get-tuple-element.31.eh_ref, bf16[2048,1024]{1,0:T(8,128)(2,1)S(1)} %get-tuple-element.32.el_ref, ...), custom_call_target="tpu_custom_call" | custom-call | flops 805306368 | bytes 8388608 | tf_op jit(solution)/shard_map/sums/pallas_call | solution.py:116
  34.0 2.2 %collective-permute-start = (f32[64,1152]{1,0:T(8,128)S(1)}, f32[64,1152]{1,0:T(8,128)S(1)}, u32[]{:S(2)}, u32[]{:S(2)}) collective-permute-start(f32[64,1152]{1,0:T(8,128)S(1)} %sums.6), channel_id=1, source_target_pairs={{0,8},{8,0},{1,9},{9,1},{2,10},{10,2},{3,11},{11,3},{4,12},{12,4},... | collective-permute-start | bytes 884744 | tf_op jit(solution)/shard_map/ppermute | solution.py:277
  36.2 3.7 %sums.8 = f32[192,1152]{1,0:T(8,128)S(1)} custom-call(s32[3]{0:T(128)S(1)} %pad_add_fusion._, f32[8,2,2048]{2,1,0:T(2,128)S(1)} %all_to_all.25.stats_ref, f32[2,2048]{1,0:T(2,128)S(1)} %get-tuple-element.30.own_ref, bf16[2048,1024]{1,0:T(8,128)(2,1)S(1)} %get-tuple-element.31.eh_ref, bf16[2048,1024]{1,0:T(8,128)(2,1)S(1)} %get-tuple-element.32.el_ref, ...), custom_call_target="tpu_custom_call" | custom-call | flops 2415919104 | bytes 8388608 | tf_op jit(solution)/shard_map/sums/pallas_call | solution.py:116
  39.9 0.1 collective-permute-start.1
  40.0 1.7 %sums.5 = f32[64,1152]{1,0:T(8,128)S(1)} custom-call(s32[1]{0:T(128)} %bitcast.1._, f32[8,2,2048]{2,1,0:T(2,128)S(1)} %all_to_all.25.stats_ref, f32[2,2048]{1,0:T(2,128)S(1)} %get-tuple-element.30.own_ref, bf16[2048,1024]{1,0:T(8,128)(2,1)S(1)} %get-tuple-element.31.eh_ref, bf16[2048,1024]{1,0:T(8,128)(2,1)S(1)} %get-tuple-element.32.el_ref, ...), custom_call_target="tpu_custom_call" | custom-call | flops 805306368 | bytes 8388608 | tf_op jit(solution)/shard_map/sums/pallas_call | solution.py:116
  41.8 1.3 collective-permute-start.2
  43.1 1.5 %collective-permute-start.3 = (f32[32,1152]{1,0:T(8,128)S(1)}, f32[32,1152]{1,0:T(8,128)S(1)}, u32[]{:S(2)}, u32[]{:S(2)}) collective-permute-start(f32[32,1152]{1,0:T(8,128)S(1)} %get-tuple-element.54), channel_id=1, source_target_pairs={{0,192},{64,0},{128,64},{192,128},{1,193},{65,1},{129,65},{193,129... | collective-permute-start | bytes 442376 | tf_op jit(solution)/shard_map/ppermute | solution.py:281
  44.6 2.8 %sums.7 = f32[128,1152]{1,0:T(8,128)S(1)} custom-call(s32[2]{0:T(128)S(1)} %pad_add_fusion.1._, f32[8,2,2048]{2,1,0:T(2,128)S(1)} %all_to_all.25.stats_ref, f32[2,2048]{1,0:T(2,128)S(1)} %get-tuple-element.30.own_ref, bf16[2048,1024]{1,0:T(8,128)(2,1)S(1)} %get-tuple-element.31.eh_ref, bf16[2048,1024]{1,0:T(8,128)(2,1)S(1)} %get-tuple-element.32.el_ref, ...), custom_call_target="tpu_custom_call" | custom-call | flops 1610612736 | bytes 8388608 | tf_op jit(solution)/shard_map/sums/pallas_call | solution.py:116
  47.4 0.0 copy-start.1
  47.4 0.0 copy-start
  47.4 0.1 slice_add_fusion
  47.5 0.6 collective-permute-done.2
  48.0 0.1 slice_add_fusion.3
  48.1 2.4 %collective-permute-start.5 = (f32[64,1152]{1,0:T(8,128)S(1)}, f32[64,1152]{1,0:T(8,128)S(1)}, u32[]{:S(2)}, u32[]{:S(2)}) collective-permute-start(f32[64,1152]{1,0:T(8,128)S(1)} %pad_maximum_fusion.1), channel_id=1, source_target_pairs={{0,192},{64,0},{128,64},{192,128},{1,193},{65,1},{129,65},{193,129... | collective-permute-start | bytes 884744 | tf_op jit(solution)/shard_map/ppermute | solution.py:281
  50.6 0.1 collective-permute-start.4
  50.7 0.1 prepare.3.c_ref
  50.8 0.5 prepare.2.c_ref
  51.3 1.7 %sums.9 = f32[64,1152]{1,0:T(8,128)S(1)} custom-call(s32[1]{0:T(128)} %bitcast.7._.slice_ref, f32[8,2,2048]{2,1,0:T(2,128)S(1)} %all_to_all.25.stats_ref, f32[2,2048]{1,0:T(2,128)S(1)} %get-tuple-element.30.own_ref, bf16[2048,1024]{1,0:T(8,128)(2,1)S(1)} %get-tuple-element.31.eh_ref, bf16[2048,1024]{1,0:T(8,128)(2,1)S(1)} %get-tuple-element.32.el_ref, ...), custom_call_target="tpu_custom_call" | custom-call | flops 805306368 | bytes 8388608 | tf_op jit(solution)/shard_map/sums/pallas_call | solution.py:116
  53.1 2.3 %collective-permute-done.5 = f32[64,1152]{1,0:T(8,128)S(1)} collective-permute-done((f32[64,1152]{1,0:T(8,128)S(1)}, f32[64,1152]{1,0:T(8,128)S(1)}, u32[]{:S(2)}, u32[]{:S(2)}) %collective-permute-start.5) | collective-permute-done | bytes 294944 | tf_op jit(solution)/shard_map/ppermute | solution.py:281
  55.4 3.1 %collective-permute-done.4 = f32[64,1152]{1,0:T(8,128)S(1)} collective-permute-done((f32[64,1152]{1,0:T(8,128)S(1)}, f32[64,1152]{1,0:T(8,128)S(1)}, u32[]{:S(2)}, u32[]{:S(2)}) %collective-permute-start.4) | collective-permute-done | bytes 294944 | tf_op jit(solution)/shard_map/ppermute | solution.py:281
  58.4 0.1 fusion.1
  58.5 9.4 %all_to_all.26.part_ref = f32[4,16,1152]{2,1,0:T(8,128)S(1)} all-to-all(f32[4,16,1152]{2,1,0:T(8,128)S(1)} %bitcast.14), channel_id=1, replica_groups=mesh['x'=4,'zl'=4,'c'=2,'zh'=2,'y'=4] {'zl'}, dimensions={0} | all-to-all | bytes 589824 | tf_op jit(solution)/shard_map/all_to_all | solution.py:327
  68.0 0.7 points.1
  68.7 0.0 collective-permute-start.8
  68.7 1.4 %collective-permute-start.7 = (f32[16,1024]{1,0:T(8,128)S(1)}, f32[16,1024]{1,0:T(8,128)S(1)}, u32[]{:S(2)}, u32[]{:S(2)}) collective-permute-start(f32[16,1024]{1,0:T(8,128)S(1)} %get-tuple-element.42), channel_id=1, source_target_pairs={{0,192},{64,128},{128,64},{192,0},{1,193},{65,129},{129,65},{193,1... | collective-permute-start | bytes 196616 | tf_op jit(solution)/shard_map/ppermute | solution.py:286
  70.0 1.3 collective-permute-start.6
  71.3 1.8 %collective-permute-done.6 = f32[16,1024]{1,0:T(8,128)S(1)} collective-permute-done((f32[16,1024]{1,0:T(8,128)S(1)}, f32[16,1024]{1,0:T(8,128)S(1)}, u32[]{:S(2)}, u32[]{:S(2)}) %collective-permute-start.6) | collective-permute-done | bytes 65568 | tf_op jit(solution)/shard_map/ppermute | solution.py:286
  73.2 0.5 collective-permute-done.7
  73.7 5.4 %collective-permute-start.9 = (f32[64,1024]{1,0:T(8,128)S(1)}, f32[64,1024]{1,0:T(8,128)S(1)}, u32[]{:S(2)}, u32[]{:S(2)}) collective-permute-start(f32[64,1024]{1,0:T(8,128)S(1)} %constant_dynamic-update-slice_fusion.own_ref), channel_id=1, source_target_pairs={{0,8},{8,0},{1,9},{9,1},{2,10},{10,2},{3,11},{11,3},{4,12},{12,4},... | collective-permute-start | bytes 786440 | tf_op jit(solution)/shard_map/ppermute | solution.py:277
  79.1 1.2 collective-permute-done.9.other_ref
  80.3 1.7 %coarse.1 = f32[64,1152]{1,0:T(8,128)S(1)} custom-call(s32[1]{0:T(128)} %bitcast.7._.slice_ref, f32[64,1024]{1,0:T(8,128)S(1)} %constant_dynamic-update-slice_fusion.own_ref, f32[64,1024]{1,0:T(8,128)S(1)} %collective-permute-done.9.other_ref, bf16[1024,1024]{1,0:T(8,128)(2,1)S(1)} %prepare.2.c_ref), custom_call_target="tpu_custom_call" | custom-call | tf_op jit(solution)/shard_map/coarse/pallas_call | solution.py:199
  82.0 0.2 reshape.25
  82.2 13.3 %all_to_all.27 = f32[32,2,1152]{2,1,0:T(2,128)S(1)} all-to-all(f32[32,2,1152]{2,1,0:T(2,128)S(1)} %reshape.25), channel_id=1, replica_groups=mesh['x'=4,'zl'=4,'c'=2,'zh'=2,'y'=4] {'y','zh','zl'}, dimensions={0} | all-to-all | bytes 589824 | tf_op jit(solution)/shard_map/all_to_all | solution.py:273
  95.4 0.1 reduce_sum.9
  95.5 0.1 slice_reduce_fusion
  95.7 0.1 slice_divide_fusion
  95.8 12.0 %all_to_all.28 = f32[8,2,1024]{2,1,0:T(2,128)S(1)} all-to-all(f32[8,2,1024]{2,1,0:T(2,128)S(1)} %broadcast_in_dim.24), channel_id=1, replica_groups=mesh['x'=4,'zl'=4,'c'=2,'zh'=2,'y'=4] {'zh','zl'}, dimensions={0} | all-to-all | bytes 131072 | tf_op jit(solution)/shard_map/all_to_all | solution.py:268
  107.8 0.1 broadcast_in_dim.26
  107.9 17.7 %all_to_all.29 = f32[16,16,1024]{2,1,0:T(8,128)S(1)} all-to-all(f32[16,16,1024]{2,1,0:T(8,128)S(1)} %broadcast_in_dim.26), channel_id=1, replica_groups=mesh['x'=4,'zl'=4,'c'=2,'zh'=2,'y'=4] {'x','y'}, dimensions={0} | all-to-all | bytes 2097152 | tf_op jit(solution)/shard_map/all_to_all | solution.py:268
  125.6 4.6 %collective-permute-start.10 = (f32[256,1024]{1,0:T(8,128)S(1)}, f32[256,1024]{1,0:T(8,128)S(1)}, u32[]{:S(2)}, u32[]{:S(2)}) collective-permute-start(f32[256,1024]{1,0:T(8,128)S(1)} %bitcast.12), channel_id=1, source_target_pairs={{0,8},{8,0},{1,9},{9,1},{2,10},{10,2},{3,11},{11,3},{4,12},{12,4},... | collective-permute-start | bytes 3145736 | tf_op jit(solution)/shard_map/ppermute | solution.py:277
  130.3 1.6 %top.1 = (f32[64,1152]{1,0:T(8,128)S(1)}, f32[512,1024]{1,0:T(8,128)}) custom-call(s32[1]{0:T(128)} %bitcast.10.core_ref, f32[256,1024]{1,0:T(8,128)S(1)} %bitcast.13, bf16[128,1024]{1,0:T(8,128)(2,1)S(1)} %prepare.3.c_ref), custom_call_target="tpu_custom_call" | custom-call | tf_op jit(solution)/shard_map/top/pallas_call | solution.py:227
  131.9 0.1 collective-permute-start.11
  132.0 1.6 %collective-permute-done.11.add_ref = f32[64,1152]{1,0:T(8,128)S(1)} collective-permute-done((f32[64,1152]{1,0:T(8,128)S(1)}, f32[64,1152]{1,0:T(8,128)S(1)}, u32[]{:S(2)}, u32[]{:S(2)}) %collective-permute-start.11) | collective-permute-done | bytes 294944 | tf_op jit(solution)/shard_map/ppermute | solution.py:277
  133.5 1.7 %final.1 = (f32[512,1024]{1,0:T(8,128)}, f32[64,1024]{1,0:T(8,128)}) custom-call(s32[1]{0:T(128)} %bitcast.10.core_ref, f32[512,1024]{1,0:T(8,128)} %get-tuple-element.45._, f32[256,1024]{1,0:T(8,128)S(1)} %collective-permute-done.10.other_ref, f32[64,1152]{1,0:T(8,128)S(1)} %get-tuple-element.46.part_ref, ...), custom_call_target="tpu_custom_call", output_to_operand_aliasing={{0}: (1, {})} | custom-call | tf_op jit(solution)/shard_map/final/pallas_call | solution.py:252
  (18 shorter events, 0.2 us)
Async XLA Ops:
  34.0 7.7 %collective-permute-start = (f32[64,1152]{1,0:T(8,128)S(1)}, f32[64,1152]{1,0:T(8,128)S(1)}, u32[]{:S(2)}, u32[]{:S(2)}) collective-permute-start(f32[64,1152]{1,0:T(8,128)S(1)} %sums.6), channel_id=1, source_target_pairs={{0,8},{8,0},{1,9},{9,1},{2,10},{10,2},{3,11},{11,3},{4,12},{12,4},... | collective-permute-start | bytes 884744 | tf_op jit(solution)/shard_map/ppermute | solution.py:277
  39.9 7.5 %collective-permute-start.1 = (f32[192,1152]{1,0:T(8,128)S(1)}, f32[192,1152]{1,0:T(8,128)S(1)}, u32[]{:S(2)}, u32[]{:S(2)}) collective-permute-start(f32[192,1152]{1,0:T(8,128)S(1)} %sums.8), channel_id=1, source_target_pairs={{0,8},{8,0},{1,9},{9,1},{2,10},{10,2},{3,11},{11,3},{4,12},{12,4},... | collective-permute-start | bytes 2654216 | tf_op jit(solution)/shard_map/ppermute | solution.py:277
  41.8 6.2 %collective-permute-start.2 = (f32[32,1152]{1,0:T(8,128)S(1)}, f32[32,1152]{1,0:T(8,128)S(1)}, u32[]{:S(2)}, u32[]{:S(2)}) collective-permute-start(f32[32,1152]{1,0:T(8,128)S(1)} %get-tuple-element.53), channel_id=1, source_target_pairs={{0,64},{64,128},{128,192},{192,0},{1,65},{65,129},{129,193},{193,1... | collective-permute-start | bytes 442376 | tf_op jit(solution)/shard_map/ppermute | solution.py:281
  43.1 4.9 %collective-permute-start.3 = (f32[32,1152]{1,0:T(8,128)S(1)}, f32[32,1152]{1,0:T(8,128)S(1)}, u32[]{:S(2)}, u32[]{:S(2)}) collective-permute-start(f32[32,1152]{1,0:T(8,128)S(1)} %get-tuple-element.54), channel_id=1, source_target_pairs={{0,192},{64,0},{128,64},{192,128},{1,193},{65,1},{129,65},{193,129... | collective-permute-start | bytes 442376 | tf_op jit(solution)/shard_map/ppermute | solution.py:281
  47.4 3.3 %copy-start.1 = (f32[64,1024]{1,0:T(8,128)S(1)}, f32[64,1024]{1,0:T(8,128)}, u32[]{:S(2)}) copy-start(f32[64,1024]{1,0:T(8,128)} %c_ref.1) | copy-start | bytes 786436
  47.4 3.5 %copy-start = (f32[512,1024]{1,0:T(8,128)S(1)}, f32[512,1024]{1,0:T(8,128)}, u32[]{:S(2)}) copy-start(f32[512,1024]{1,0:T(8,128)} %c_ref) | copy-start | bytes 6291460
  48.1 7.3 %collective-permute-start.5 = (f32[64,1152]{1,0:T(8,128)S(1)}, f32[64,1152]{1,0:T(8,128)S(1)}, u32[]{:S(2)}, u32[]{:S(2)}) collective-permute-start(f32[64,1152]{1,0:T(8,128)S(1)} %pad_maximum_fusion.1), channel_id=1, source_target_pairs={{0,192},{64,0},{128,64},{192,128},{1,193},{65,1},{129,65},{193,129... | collective-permute-start | bytes 884744 | tf_op jit(solution)/shard_map/ppermute | solution.py:281
  50.6 7.9 %collective-permute-start.4 = (f32[64,1152]{1,0:T(8,128)S(1)}, f32[64,1152]{1,0:T(8,128)S(1)}, u32[]{:S(2)}, u32[]{:S(2)}) collective-permute-start(f32[64,1152]{1,0:T(8,128)S(1)} %pad_maximum_fusion), channel_id=1, source_target_pairs={{0,64},{64,128},{128,192},{192,0},{1,65},{65,129},{129,193},{193,1... | collective-permute-start | bytes 884744 | tf_op jit(solution)/shard_map/ppermute | solution.py:281
  68.7 5.0 %collective-permute-start.8 = (f32[16,1024]{1,0:T(8,128)S(1)}, f32[16,1024]{1,0:T(8,128)S(1)}, u32[]{:S(2)}, u32[]{:S(2)}) collective-permute-start(f32[16,1024]{1,0:T(8,128)S(1)} %get-tuple-element.42), channel_id=1, source_target_pairs={{0,128},{64,192},{128,0},{192,64},{1,129},{65,193},{129,1},{193,65... | collective-permute-start | bytes 196616 | tf_op jit(solution)/shard_map/ppermute | solution.py:286
  68.7 5.0 %collective-permute-start.7 = (f32[16,1024]{1,0:T(8,128)S(1)}, f32[16,1024]{1,0:T(8,128)S(1)}, u32[]{:S(2)}, u32[]{:S(2)}) collective-permute-start(f32[16,1024]{1,0:T(8,128)S(1)} %get-tuple-element.42), channel_id=1, source_target_pairs={{0,192},{64,128},{128,64},{192,0},{1,193},{65,129},{129,65},{193,1... | collective-permute-start | bytes 196616 | tf_op jit(solution)/shard_map/ppermute | solution.py:286
  70.0 3.1 %collective-permute-start.6 = (f32[16,1024]{1,0:T(8,128)S(1)}, f32[16,1024]{1,0:T(8,128)S(1)}, u32[]{:S(2)}, u32[]{:S(2)}) collective-permute-start(f32[16,1024]{1,0:T(8,128)S(1)} %get-tuple-element.42), channel_id=1, source_target_pairs={{0,64},{64,0},{128,192},{192,128},{1,65},{65,1},{129,193},{193,129... | collective-permute-start | bytes 196616 | tf_op jit(solution)/shard_map/ppermute | solution.py:286
  73.7 6.6 %collective-permute-start.9 = (f32[64,1024]{1,0:T(8,128)S(1)}, f32[64,1024]{1,0:T(8,128)S(1)}, u32[]{:S(2)}, u32[]{:S(2)}) collective-permute-start(f32[64,1024]{1,0:T(8,128)S(1)} %constant_dynamic-update-slice_fusion.own_ref), channel_id=1, source_target_pairs={{0,8},{8,0},{1,9},{9,1},{2,10},{10,2},{3,11},{11,3},{4,12},{12,4},... | collective-permute-start | bytes 786440 | tf_op jit(solution)/shard_map/ppermute | solution.py:277
  125.6 7.9 %collective-permute-start.10 = (f32[256,1024]{1,0:T(8,128)S(1)}, f32[256,1024]{1,0:T(8,128)S(1)}, u32[]{:S(2)}, u32[]{:S(2)}) collective-permute-start(f32[256,1024]{1,0:T(8,128)S(1)} %bitcast.12), channel_id=1, source_target_pairs={{0,8},{8,0},{1,9},{9,1},{2,10},{10,2},{3,11},{11,3},{4,12},{12,4},... | collective-permute-start | bytes 3145736 | tf_op jit(solution)/shard_map/ppermute | solution.py:277
  131.9 1.7 %collective-permute-start.11 = (f32[64,1152]{1,0:T(8,128)S(1)}, f32[64,1152]{1,0:T(8,128)S(1)}, u32[]{:S(2)}, u32[]{:S(2)}) collective-permute-start(f32[64,1152]{1,0:T(8,128)S(1)} %get-tuple-element.46.part_ref), channel_id=1, source_target_pairs={{0,8},{8,0},{1,9},{9,1},{2,10},{10,2},{3,11},{11,3},{4,12},{12,4},... | collective-permute-start | bytes 884744 | tf_op jit(solution)/shard_map/ppermute | solution.py:277

commit v5 on v4

--- a/solution.py
+++ b/solution.py
@@ -104,14 +104,22 @@
     wh, wl = split(w)
     both = mm(jnp.concatenate([wh, wl], axis=0), eh_ref[here, :], NN)
     part = both[:k] + both[k:] + mm(wh, el_ref[here, :], NN)
-    mass = jnp.broadcast_to(jnp.sum(w, axis=1, keepdims=True), (k, MASS))
-    o_ref[:, :d] += part
-    o_ref[:, d:] += mass
+    mass = jnp.sum(w, axis=1, keepdims=True)
+    lane = lax.broadcasted_iota(jnp.int32, (8, 128), 1)
+    tile = 0
+    for row in range(0, k, 16):
+        for first in (row, row + 8):
+            for column in range(0, d, 128):
+                o_ref[tile] += part[first : first + 8, column : column + 128]
+                tile += 1
+        o_ref[tile] += jnp.where(lane == 0, mass[row : row + 8], mass[row + 8 : row + 16])
+        tile += 1
 
 
 def sums(stats, own, p, eh, el, blocks, rows=64, block=1024):
     n, d = eh.shape
     count = blocks.shape[0]
+    tiles = rows * count // 16 * (2 * d // 128 + 1)
     whole = pl.BlockSpec(memory_space=pltpu.VMEM)
     return pl.pallas_call(
         sums_kernel,
@@ -125,9 +133,9 @@
                 whole,
             ]
             + [pl.BlockSpec((rows, block), lambda i, b, j=j: (b[j], i)) for j in range(count)],
-            out_specs=pl.BlockSpec((rows * count, d + MASS), lambda i, b: (0, 0)),
+            out_specs=pl.BlockSpec((tiles, 8, 128), lambda i, b: (0, 0, 0)),
         ),
-        out_shape=jax.ShapeDtypeStruct((rows * count, d + MASS), F32),
+        out_shape=jax.ShapeDtypeStruct((tiles, 8, 128), F32),
         compiler_params=pltpu.CompilerParams(vmem_limit_bytes=VMEM),
         cost_estimate=pl.CostEstimate(flops=6 * n * d * rows * count, bytes_accessed=4 * n * d, transcendentals=0),
         name="sums",
@@ -168,18 +176,20 @@
 
 
 def points_kernel(part_ref, fine_ref, points_ref):
-    part = part_ref[0] + part_ref[1] + part_ref[2] + part_ref[3]
     d = fine_ref.shape[1]
-    fine = part[:, :d] / part[:, d : d + 1]
-    fine_ref[...] = fine
-    points_ref[...] = unit_rms(fine)
-
-
-def points_of(part):
-    _, n, d = part.shape
+    mass = sum(part_ref[i, 2 * d // 128] for i in range(4))
+    for half in range(2):
+        first = half * (d // 128)
+        tiles = [sum(part_ref[i, first + j] for i in range(4)) for j in range(d // 128)]
+        fine = jnp.concatenate(tiles, axis=1) / mass[:, half : half + 1]
+        fine_ref[half * 8 : half * 8 + 8, :] = fine
+        points_ref[half * 8 : half * 8 + 8, :] = unit_rms(fine)
+
+
+def points_of(part, d):
     return pl.pallas_call(
         points_kernel,
-        out_shape=[jax.ShapeDtypeStruct((n, d - MASS), F32)] * 2,
+        out_shape=[jax.ShapeDtypeStruct((16, d), F32)] * 2,
         compiler_params=pltpu.CompilerParams(vmem_limit_bytes=VMEM),
         name="points",
     )(part)
@@ -312,19 +322,19 @@
     far_own = sums(stats, own, p, eh, el, blocks[1])
     near_in = swap_core(sums(stats, own, p, eh, el, blocks[2]))
     far_sum = far_own + far_in
-    up_part, down_part = shift(far_sum[:32], 1), shift(far_sum[32:], -1)
+    up_part, down_part = shift(far_sum[:34], 1), shift(far_sum[34:], -1)
     blocks[3], _ = lax.optimization_barrier((blocks[3], far_sum))
-    near = sums(stats, own, p, eh, el, blocks[3]) + near_in[:128]
-    up_sum = jnp.concatenate([near[:32] + up_part, near[32:64]], axis=0)
-    down_sum = jnp.concatenate([near[64:96], near[96:] + down_part], axis=0)
+    near = sums(stats, own, p, eh, el, blocks[3]) + near_in[:136]
+    up_sum = jnp.concatenate([near[:34] + up_part, near[34:68]], axis=0)
+    down_sum = jnp.concatenate([near[68:102], near[102:] + down_part], axis=0)
     from_down, from_up = shift(up_sum, 1), shift(down_sum, -1)
     blocks[4], _ = lax.optimization_barrier((blocks[4], (up_sum, down_sum)))
     part = sums(stats, own, p, eh, el, blocks[4])
-    part = part + near_in[128:] + from_down + from_up
+    part = part + near_in[136:] + from_down + from_up
     coarse_centroids, top_centroids, _ = lax.optimization_barrier((coarse_centroids, top_centroids, up_sum))
     coarse_centers, top_centers = prepare(coarse_centroids), prepare(top_centroids)
     part, coarse_centers, top_centers = lax.optimization_barrier((part, coarse_centers, top_centers))
-    fine, points = points_of(lax.all_to_all(part.reshape(4, 16, dim + MASS), "zl", 0, 0))
+    fine, points = points_of(lax.all_to_all(part.reshape(4, 17, 8, 128), "zl", 0, 0), dim)
 
     points = jnp.concatenate([points, *trade([points] * 3, "x")], axis=0)
     part = coarse_sums((core * 4 + x).reshape(1), points, swap_core(points), coarse_centers, 64)

time: 136 us -> 135 us (level)
  transfers between devices with their start and end apart: 12 -> 12, of which waited for: 7 -> 7; matrix products, arithmetic and copies ran while one was open for 0% -> 0% of each run, Pallas kernels for 9% -> 8%
where the time goes in v5:
time: 135 us
  blocking collectives  73.4 us (54%)
  Pallas kernels  28.5 us (21%)
  starting transfers between devices  20 us (15%)
  waiting for transfers between devices  10.5 us (8%)
    all_to_all x3, blocking collectives, spread(): lax.all_to_all(jnp.broadcast_to(value[None], (size, *value.shape)), axes,...  50.8 us
    all_to_all x1, blocking collectives, add_up(): return jnp.sum(lax.all_to_all(part, axes, 0, 0), axis=0)  13.3 us
    ppermute x5, starting transfers between devices, swap_core(): return lax.ppermute(value, 'c', [(0, 1), (1, 0)])  12 us
    pallas_call x5, Pallas kernels, sums(): pl.pallas_call(sums_kernel, grid_spec=pltpu.PrefetchScalarGridSpec(num_sc...  11.6 us
    pallas_call x1, Pallas kernels, fit(): pl.pallas_call(functools.partial(fit_kernel, step), in_specs=[pl.BlockSpe...  10.6 us
    all_to_all x1, blocking collectives, body(): lax.all_to_all(part.reshape(4, 17, 8, 128), 'zl', 0, 0)  9.38 us
    ppermute x4, waiting for transfers between devices, shift(): return lax.ppermute(value, 'x', [(i, (i + step) % 4) for i in range(4)])  5.44 us
    ppermute x4, starting transfers between devices, shift(): return lax.ppermute(value, 'x', [(i, (i + step) % 4) for i in range(4)])  5.27 us
  transfers between devices with their start and end apart: 12, of which 7 were waited for; matrix products, arithmetic and copies ran while one was open for 0% of the time, Pallas kernels for 8%

profile of v5, /device:TPU:1, one launch (start us, length us, event | category | flops | bytes accessed | tf_op | source)
XLA Modules:
  0.0 134.7 jit_solution(11881127925226814288)
XLA Ops:
  0.7 0.1 pad_add_fusion.1._
  0.7 10.6 %fit.1 = (f32[512,2048]{1,0:T(8,128)S(1)}, f32[2,2048]{1,0:T(2,128)S(1)}, bf16[2048,1024]{1,0:T(8,128)(2,1)S(1)}, bf16[2048,1024]{1,0:T(8,128)(2,1)S(1)}) custom-call(f32[2048,1024]{1,0:T(8,128)} %e_hbm.1, f32[512,1024]{1,0:T(8,128)} %c_hbm.1), custom_call_target="tpu_custom_call" | custom-call | tf_op jit(solution)/shard_map/fit/pallas_call | solution.py:69
  11.4 0.1 pad_add_fusion._
  11.5 20.8 %all_to_all.25.stats_ref = f32[8,2,2048]{2,1,0:T(2,128)S(1)} all-to-all(f32[8,2,2048]{2,1,0:T(2,128)S(1)} %broadcast_in_dim.10), channel_id=1, replica_groups=mesh['x'=4,'zl'=4,'c'=2,'zh'=2,'y'=4] {'zh','y'}, dimensions={0} | all-to-all | bytes 262144 | tf_op jit(solution)/shard_map/all_to_all | solution.py:278
  32.3 3.6 %sums.8 = f32[204,8,128]{2,1,0:T(8,128)S(1)} custom-call(s32[3]{0:T(128)S(1)} %pad_add_fusion._, f32[8,2,2048]{2,1,0:T(2,128)S(1)} %all_to_all.25.stats_ref, f32[2,2048]{1,0:T(2,128)S(1)} %get-tuple-element.30.own_ref, bf16[2048,1024]{1,0:T(8,128)(2,1)S(1)} %get-tuple-element.31.eh_ref, bf16[2048,1024]{1,0:T(8,128)(2,1)S(1)} %get-tuple-element.32.el_ref, ...), custom_call_target="tpu_custom_call" | custom-call | flops 2415919104 | bytes 8388608 | tf_op jit(solution)/shard_map/sums/pallas_call | solution.py:124
  35.9 2.2 %collective-permute-start.1 = (f32[204,8,128]{2,1,0:T(8,128)S(1)}, f32[204,8,128]{2,1,0:T(8,128)S(1)}, u32[]{:S(2)}, u32[]{:S(2)}) collective-permute-start(f32[204,8,128]{2,1,0:T(8,128)S(1)} %sums.8), channel_id=1, source_target_pairs={{0,8},{8,0},{1,9},{9,1},{2,10},{10,2},{3,11},{11,3},{4,12},{12,4},... | collective-permute-start | bytes 2506760 | tf_op jit(solution)/shard_map/ppermute | solution.py:287
  38.1 1.7 %sums.6 = f32[68,8,128]{2,1,0:T(8,128)S(1)} custom-call(s32[1]{0:T(128)} %bitcast._, f32[8,2,2048]{2,1,0:T(2,128)S(1)} %all_to_all.25.stats_ref, f32[2,2048]{1,0:T(2,128)S(1)} %get-tuple-element.30.own_ref, bf16[2048,1024]{1,0:T(8,128)(2,1)S(1)} %get-tuple-element.31.eh_ref, bf16[2048,1024]{1,0:T(8,128)(2,1)S(1)} %get-tuple-element.32.el_ref, ...), custom_call_target="tpu_custom_call" | custom-call | flops 805306368 | bytes 8388608 | tf_op jit(solution)/shard_map/sums/pallas_call | solution.py:124
  39.9 0.1 collective-permute-start
  40.0 1.7 %sums.5 = f32[68,8,128]{2,1,0:T(8,128)S(1)} custom-call(s32[1]{0:T(128)} %bitcast.1._, f32[8,2,2048]{2,1,0:T(2,128)S(1)} %all_to_all.25.stats_ref, f32[2,2048]{1,0:T(2,128)S(1)} %get-tuple-element.30.own_ref, bf16[2048,1024]{1,0:T(8,128)(2,1)S(1)} %get-tuple-element.31.eh_ref, bf16[2048,1024]{1,0:T(8,128)(2,1)S(1)} %get-tuple-element.32.el_ref, ...), custom_call_target="tpu_custom_call" | custom-call | flops 805306368 | bytes 8388608 | tf_op jit(solution)/shard_map/sums/pallas_call | solution.py:124
  41.8 1.3 collective-permute-start.2
  43.1 1.5 %collective-permute-start.3 = (f32[34,8,128]{2,1,0:T(8,128)S(1)}, f32[34,8,128]{2,1,0:T(8,128)S(1)}, u32[]{:S(2)}, u32[]{:S(2)}) collective-permute-start(f32[34,8,128]{2,1,0:T(8,128)S(1)} %get-tuple-element.54), channel_id=1, source_target_pairs={{0,192},{64,0},{128,64},{192,128},{1,193},{65,1},{129,65},{193,129... | collective-permute-start | bytes 417800 | tf_op jit(solution)/shard_map/ppermute | solution.py:291
  44.6 2.8 %sums.7 = f32[136,8,128]{2,1,0:T(8,128)S(1)} custom-call(s32[2]{0:T(128)S(1)} %pad_add_fusion.1._, f32[8,2,2048]{2,1,0:T(2,128)S(1)} %all_to_all.25.stats_ref, f32[2,2048]{1,0:T(2,128)S(1)} %get-tuple-element.30.own_ref, bf16[2048,1024]{1,0:T(8,128)(2,1)S(1)} %get-tuple-element.31.eh_ref, bf16[2048,1024]{1,0:T(8,128)(2,1)S(1)} %get-tuple-element.32.el_ref, ...), custom_call_target="tpu_custom_call" | custom-call | flops 1610612736 | bytes 8388608 | tf_op jit(solution)/shard_map/sums/pallas_call | solution.py:124
  47.3 0.0 copy-start.1
  47.4 0.0 copy-start
  47.4 0.1 slice_add_fusion
  47.5 0.4 collective-permute-done.2
  47.9 0.1 slice_add_fusion.3
  48.0 2.4 %collective-permute-start.5 = (f32[68,8,128]{2,1,0:T(8,128)S(1)}, f32[68,8,128]{2,1,0:T(8,128)S(1)}, u32[]{:S(2)}, u32[]{:S(2)}) collective-permute-start(f32[68,8,128]{2,1,0:T(8,128)S(1)} %pad_maximum_fusion.1), channel_id=1, source_target_pairs={{0,192},{64,0},{128,64},{192,128},{1,193},{65,1},{129,65},{193,129... | collective-permute-start | bytes 835592 | tf_op jit(solution)/shard_map/ppermute | solution.py:291
  50.4 0.1 collective-permute-start.4
  50.5 0.1 prepare.3.c_ref
  50.7 0.5 prepare.2.c_ref
  51.2 1.7 %sums.9 = f32[68,8,128]{2,1,0:T(8,128)S(1)} custom-call(s32[1]{0:T(128)} %bitcast.7._.slice_ref, f32[8,2,2048]{2,1,0:T(2,128)S(1)} %all_to_all.25.stats_ref, f32[2,2048]{1,0:T(2,128)S(1)} %get-tuple-element.30.own_ref, bf16[2048,1024]{1,0:T(8,128)(2,1)S(1)} %get-tuple-element.31.eh_ref, bf16[2048,1024]{1,0:T(8,128)(2,1)S(1)} %get-tuple-element.32.el_ref, ...), custom_call_target="tpu_custom_call" | custom-call | flops 805306368 | bytes 8388608 | tf_op jit(solution)/shard_map/sums/pallas_call | solution.py:124
  52.9 2.0 %collective-permute-done.5 = f32[68,8,128]{2,1,0:T(8,128)S(1)} collective-permute-done((f32[68,8,128]{2,1,0:T(8,128)S(1)}, f32[68,8,128]{2,1,0:T(8,128)S(1)}, u32[]{:S(2)}, u32[]{:S(2)}) %collective-permute-start.5) | collective-permute-done | bytes 278560 | tf_op jit(solution)/shard_map/ppermute | solution.py:291
  54.9 3.1 %collective-permute-done.4 = f32[68,8,128]{2,1,0:T(8,128)S(1)} collective-permute-done((f32[68,8,128]{2,1,0:T(8,128)S(1)}, f32[68,8,128]{2,1,0:T(8,128)S(1)}, u32[]{:S(2)}, u32[]{:S(2)}) %collective-permute-start.4) | collective-permute-done | bytes 278560 | tf_op jit(solution)/shard_map/ppermute | solution.py:291
  57.9 0.1 fusion.1
  58.0 9.4 %all_to_all.26.part_ref = f32[4,17,8,128]{3,2,1,0:T(8,128)S(1)} all-to-all(f32[4,17,8,128]{3,2,1,0:T(8,128)S(1)} %bitcast.14), channel_id=1, replica_groups=mesh['x'=4,'zl'=4,'c'=2,'zh'=2,'y'=4] {'zl'}, dimensions={0} | all-to-all | bytes 557056 | tf_op jit(solution)/shard_map/all_to_all | solution.py:337
  67.4 0.7 points.1
  68.1 0.0 collective-permute-start.8
  68.1 1.5 %collective-permute-start.7 = (f32[16,1024]{1,0:T(8,128)S(1)}, f32[16,1024]{1,0:T(8,128)S(1)}, u32[]{:S(2)}, u32[]{:S(2)}) collective-permute-start(f32[16,1024]{1,0:T(8,128)S(1)} %get-tuple-element.42), channel_id=1, source_target_pairs={{0,192},{64,128},{128,64},{192,0},{1,193},{65,129},{129,65},{193,1... | collective-permute-start | bytes 196616 | tf_op jit(solution)/shard_map/ppermute | solution.py:296
  69.6 1.2 collective-permute-start.6
  70.8 1.9 %collective-permute-done.6 = f32[16,1024]{1,0:T(8,128)S(1)} collective-permute-done((f32[16,1024]{1,0:T(8,128)S(1)}, f32[16,1024]{1,0:T(8,128)S(1)}, u32[]{:S(2)}, u32[]{:S(2)}) %collective-permute-start.6) | collective-permute-done | bytes 65568 | tf_op jit(solution)/shard_map/ppermute | solution.py:296
  72.7 0.4 collective-permute-done.7
  73.2 5.4 %collective-permute-start.9 = (f32[64,1024]{1,0:T(8,128)S(1)}, f32[64,1024]{1,0:T(8,128)S(1)}, u32[]{:S(2)}, u32[]{:S(2)}) collective-permute-start(f32[64,1024]{1,0:T(8,128)S(1)} %constant_dynamic-update-slice_fusion.own_ref), channel_id=1, source_target_pairs={{0,8},{8,0},{1,9},{9,1},{2,10},{10,2},{3,11},{11,3},{4,12},{12,4},... | collective-permute-start | bytes 786440 | tf_op jit(solution)/shard_map/ppermute | solution.py:287
  78.6 1.2 collective-permute-done.9.other_ref
  79.8 1.7 %coarse.1 = f32[64,1152]{1,0:T(8,128)S(1)} custom-call(s32[1]{0:T(128)} %bitcast.7._.slice_ref, f32[64,1024]{1,0:T(8,128)S(1)} %constant_dynamic-update-slice_fusion.own_ref, f32[64,1024]{1,0:T(8,128)S(1)} %collective-permute-done.9.other_ref, bf16[1024,1024]{1,0:T(8,128)(2,1)S(1)} %prepare.2.c_ref), custom_call_target="tpu_custom_call" | custom-call | tf_op jit(solution)/shard_map/coarse/pallas_call | solution.py:209
  81.4 0.2 reshape.25
  81.6 13.3 %all_to_all.27 = f32[32,2,1152]{2,1,0:T(2,128)S(1)} all-to-all(f32[32,2,1152]{2,1,0:T(2,128)S(1)} %reshape.25), channel_id=1, replica_groups=mesh['x'=4,'zl'=4,'c'=2,'zh'=2,'y'=4] {'y','zh','zl'}, dimensions={0} | all-to-all | bytes 589824 | tf_op jit(solution)/shard_map/all_to_all | solution.py:283
  94.9 0.1 reduce_sum.9
  95.0 0.1 slice_reduce_fusion
  95.1 0.1 slice_divide_fusion
  95.2 11.9 %all_to_all.28 = f32[8,2,1024]{2,1,0:T(2,128)S(1)} all-to-all(f32[8,2,1024]{2,1,0:T(2,128)S(1)} %broadcast_in_dim.24), channel_id=1, replica_groups=mesh['x'=4,'zl'=4,'c'=2,'zh'=2,'y'=4] {'zh','zl'}, dimensions={0} | all-to-all | bytes 131072 | tf_op jit(solution)/shard_map/all_to_all | solution.py:278
  107.1 0.1 broadcast_in_dim.26
  107.3 18.1 %all_to_all.29 = f32[16,16,1024]{2,1,0:T(8,128)S(1)} all-to-all(f32[16,16,1024]{2,1,0:T(8,128)S(1)} %broadcast_in_dim.26), channel_id=1, replica_groups=mesh['x'=4,'zl'=4,'c'=2,'zh'=2,'y'=4] {'x','y'}, dimensions={0} | all-to-all | bytes 2097152 | tf_op jit(solution)/shard_map/all_to_all | solution.py:278
  125.4 4.2 %collective-permute-start.10 = (f32[256,1024]{1,0:T(8,128)S(1)}, f32[256,1024]{1,0:T(8,128)S(1)}, u32[]{:S(2)}, u32[]{:S(2)}) collective-permute-start(f32[256,1024]{1,0:T(8,128)S(1)} %bitcast.12), channel_id=1, source_target_pairs={{0,8},{8,0},{1,9},{9,1},{2,10},{10,2},{3,11},{11,3},{4,12},{12,4},... | collective-permute-start | bytes 3145736 | tf_op jit(solution)/shard_map/ppermute | solution.py:287
  129.6 1.6 %top.1 = (f32[64,1152]{1,0:T(8,128)S(1)}, f32[512,1024]{1,0:T(8,128)}) custom-call(s32[1]{0:T(128)} %bitcast.10.core_ref, f32[256,1024]{1,0:T(8,128)S(1)} %bitcast.13, bf16[128,1024]{1,0:T(8,128)(2,1)S(1)} %prepare.3.c_ref), custom_call_target="tpu_custom_call" | custom-call | tf_op jit(solution)/shard_map/top/pallas_call | solution.py:237
  131.2 0.1 collective-permute-start.11
  131.3 1.6 %collective-permute-done.11.add_ref = f32[64,1152]{1,0:T(8,128)S(1)} collective-permute-done((f32[64,1152]{1,0:T(8,128)S(1)}, f32[64,1152]{1,0:T(8,128)S(1)}, u32[]{:S(2)}, u32[]{:S(2)}) %collective-permute-start.11) | collective-permute-done | bytes 294944 | tf_op jit(solution)/shard_map/ppermute | solution.py:287
  132.9 1.7 %final.1 = (f32[512,1024]{1,0:T(8,128)}, f32[64,1024]{1,0:T(8,128)}) custom-call(s32[1]{0:T(128)} %bitcast.10.core_ref, f32[512,1024]{1,0:T(8,128)} %get-tuple-element.45._, f32[256,1024]{1,0:T(8,128)S(1)} %collective-permute-done.10.other_ref, f32[64,1152]{1,0:T(8,128)S(1)} %get-tuple-element.46.part_ref, ...), custom_call_target="tpu_custom_call", output_to_operand_aliasing={{0}: (1, {})} | custom-call | tf_op jit(solution)/shard_map/final/pallas_call | solution.py:262
  (18 shorter events, 0.2 us)
Async XLA Ops:
  35.9 11.4 %collective-permute-start.1 = (f32[204,8,128]{2,1,0:T(8,128)S(1)}, f32[204,8,128]{2,1,0:T(8,128)S(1)}, u32[]{:S(2)}, u32[]{:S(2)}) collective-permute-start(f32[204,8,128]{2,1,0:T(8,128)S(1)} %sums.8), channel_id=1, source_target_pairs={{0,8},{8,0},{1,9},{9,1},{2,10},{10,2},{3,11},{11,3},{4,12},{12,4},... | collective-permute-start | bytes 2506760 | tf_op jit(solution)/shard_map/ppermute | solution.py:287
  39.9 1.9 %collective-permute-start = (f32[68,8,128]{2,1,0:T(8,128)S(1)}, f32[68,8,128]{2,1,0:T(8,128)S(1)}, u32[]{:S(2)}, u32[]{:S(2)}) collective-permute-start(f32[68,8,128]{2,1,0:T(8,128)S(1)} %sums.6), channel_id=1, source_target_pairs={{0,8},{8,0},{1,9},{9,1},{2,10},{10,2},{3,11},{11,3},{4,12},{12,4},... | collective-permute-start | bytes 835592 | tf_op jit(solution)/shard_map/ppermute | solution.py:287
  41.8 6.1 %collective-permute-start.2 = (f32[34,8,128]{2,1,0:T(8,128)S(1)}, f32[34,8,128]{2,1,0:T(8,128)S(1)}, u32[]{:S(2)}, u32[]{:S(2)}) collective-permute-start(f32[34,8,128]{2,1,0:T(8,128)S(1)} %get-tuple-element.53), channel_id=1, source_target_pairs={{0,64},{64,128},{128,192},{192,0},{1,65},{65,129},{129,193},{193,1... | collective-permute-start | bytes 417800 | tf_op jit(solution)/shard_map/ppermute | solution.py:291
  43.1 4.8 %collective-permute-start.3 = (f32[34,8,128]{2,1,0:T(8,128)S(1)}, f32[34,8,128]{2,1,0:T(8,128)S(1)}, u32[]{:S(2)}, u32[]{:S(2)}) collective-permute-start(f32[34,8,128]{2,1,0:T(8,128)S(1)} %get-tuple-element.54), channel_id=1, source_target_pairs={{0,192},{64,0},{128,64},{192,128},{1,193},{65,1},{129,65},{193,129... | collective-permute-start | bytes 417800 | tf_op jit(solution)/shard_map/ppermute | solution.py:291
  47.3 3.2 %copy-start.1 = (f32[64,1024]{1,0:T(8,128)S(1)}, f32[64,1024]{1,0:T(8,128)}, u32[]{:S(2)}) copy-start(f32[64,1024]{1,0:T(8,128)} %c_ref.1) | copy-start | bytes 786436
  47.4 3.3 %copy-start = (f32[512,1024]{1,0:T(8,128)S(1)}, f32[512,1024]{1,0:T(8,128)}, u32[]{:S(2)}) copy-start(f32[512,1024]{1,0:T(8,128)} %c_ref) | copy-start | bytes 6291460
  48.0 6.9 %collective-permute-start.5 = (f32[68,8,128]{2,1,0:T(8,128)S(1)}, f32[68,8,128]{2,1,0:T(8,128)S(1)}, u32[]{:S(2)}, u32[]{:S(2)}) collective-permute-start(f32[68,8,128]{2,1,0:T(8,128)S(1)} %pad_maximum_fusion.1), channel_id=1, source_target_pairs={{0,192},{64,0},{128,64},{192,128},{1,193},{65,1},{129,65},{193,129... | collective-permute-start | bytes 835592 | tf_op jit(solution)/shard_map/ppermute | solution.py:291
  50.4 7.5 %collective-permute-start.4 = (f32[68,8,128]{2,1,0:T(8,128)S(1)}, f32[68,8,128]{2,1,0:T(8,128)S(1)}, u32[]{:S(2)}, u32[]{:S(2)}) collective-permute-start(f32[68,8,128]{2,1,0:T(8,128)S(1)} %pad_maximum_fusion), channel_id=1, source_target_pairs={{0,64},{64,128},{128,192},{192,0},{1,65},{65,129},{129,193},{193,1... | collective-permute-start | bytes 835592 | tf_op jit(solution)/shard_map/ppermute | solution.py:291
  68.1 5.0 %collective-permute-start.8 = (f32[16,1024]{1,0:T(8,128)S(1)}, f32[16,1024]{1,0:T(8,128)S(1)}, u32[]{:S(2)}, u32[]{:S(2)}) collective-permute-start(f32[16,1024]{1,0:T(8,128)S(1)} %get-tuple-element.42), channel_id=1, source_target_pairs={{0,128},{64,192},{128,0},{192,64},{1,129},{65,193},{129,1},{193,65... | collective-permute-start | bytes 196616 | tf_op jit(solution)/shard_map/ppermute | solution.py:296
  68.1 5.0 %collective-permute-start.7 = (f32[16,1024]{1,0:T(8,128)S(1)}, f32[16,1024]{1,0:T(8,128)S(1)}, u32[]{:S(2)}, u32[]{:S(2)}) collective-permute-start(f32[16,1024]{1,0:T(8,128)S(1)} %get-tuple-element.42), channel_id=1, source_target_pairs={{0,192},{64,128},{128,64},{192,0},{1,193},{65,129},{129,65},{193,1... | collective-permute-start | bytes 196616 | tf_op jit(solution)/shard_map/ppermute | solution.py:296
  69.6 3.1 %collective-permute-start.6 = (f32[16,1024]{1,0:T(8,128)S(1)}, f32[16,1024]{1,0:T(8,128)S(1)}, u32[]{:S(2)}, u32[]{:S(2)}) collective-permute-start(f32[16,1024]{1,0:T(8,128)S(1)} %get-tuple-element.42), channel_id=1, source_target_pairs={{0,64},{64,0},{128,192},{192,128},{1,65},{65,1},{129,193},{193,129... | collective-permute-start | bytes 196616 | tf_op jit(solution)/shard_map/ppermute | solution.py:296
  73.2 6.6 %collective-permute-start.9 = (f32[64,1024]{1,0:T(8,128)S(1)}, f32[64,1024]{1,0:T(8,128)S(1)}, u32[]{:S(2)}, u32[]{:S(2)}) collective-permute-start(f32[64,1024]{1,0:T(8,128)S(1)} %constant_dynamic-update-slice_fusion.own_ref), channel_id=1, source_target_pairs={{0,8},{8,0},{1,9},{9,1},{2,10},{10,2},{3,11},{11,3},{4,12},{12,4},... | collective-permute-start | bytes 786440 | tf_op jit(solution)/shard_map/ppermute | solution.py:287
  125.4 7.5 %collective-permute-start.10 = (f32[256,1024]{1,0:T(8,128)S(1)}, f32[256,1024]{1,0:T(8,128)S(1)}, u32[]{:S(2)}, u32[]{:S(2)}) collective-permute-start(f32[256,1024]{1,0:T(8,128)S(1)} %bitcast.12), channel_id=1, source_target_pairs={{0,8},{8,0},{1,9},{9,1},{2,10},{10,2},{3,11},{11,3},{4,12},{12,4},... | collective-permute-start | bytes 3145736 | tf_op jit(solution)/shard_map/ppermute | solution.py:287
  131.2 1.7 %collective-permute-start.11 = (f32[64,1152]{1,0:T(8,128)S(1)}, f32[64,1152]{1,0:T(8,128)S(1)}, u32[]{:S(2)}, u32[]{:S(2)}) collective-permute-start(f32[64,1152]{1,0:T(8,128)S(1)} %get-tuple-element.46.part_ref), channel_id=1, source_target_pairs={{0,8},{8,0},{1,9},{9,1},{2,10},{10,2},{3,11},{11,3},{4,12},{12,4},... | collective-permute-start | bytes 884744 | tf_op jit(solution)/shard_map/ppermute | solution.py:287

commit v6 on v5

--- a/solution.py
+++ b/solution.py
@@ -309,8 +309,7 @@
     blocks = [
         jnp.stack(group)
         for group in (
-            (theirs + far,),
-            (mine + far,),
+            (theirs + far, mine + far),
             (theirs + up, theirs + down, theirs + x),
             (mine + up, mine + down),
             (mine + x,),
@@ -318,18 +317,19 @@
     ]
     own, blocks = lax.optimization_barrier((own, blocks))
     stats = spread(own, CENT, 8)
-    far_in = swap_core(sums(stats, own, p, eh, el, blocks[0]))
-    far_own = sums(stats, own, p, eh, el, blocks[1])
-    near_in = swap_core(sums(stats, own, p, eh, el, blocks[2]))
+    both = sums(stats, own, p, eh, el, blocks[0])
+    far_in, far_own = swap_core(both[:68]), both[68:]
+    blocks[1], _ = lax.optimization_barrier((blocks[1], both))
+    near_in = swap_core(sums(stats, own, p, eh, el, blocks[1]))
     far_sum = far_own + far_in
     up_part, down_part = shift(far_sum[:34], 1), shift(far_sum[34:], -1)
-    blocks[3], _ = lax.optimization_barrier((blocks[3], far_sum))
-    near = sums(stats, own, p, eh, el, blocks[3]) + near_in[:136]
+    blocks[2], _ = lax.optimization_barrier((blocks[2], far_sum))
+    near = sums(stats, own, p, eh, el, blocks[2]) + near_in[:136]
     up_sum = jnp.concatenate([near[:34] + up_part, near[34:68]], axis=0)
     down_sum = jnp.concatenate([near[68:102], near[102:] + down_part], axis=0)
     from_down, from_up = shift(up_sum, 1), shift(down_sum, -1)
-    blocks[4], _ = lax.optimization_barrier((blocks[4], (up_sum, down_sum)))
-    part = sums(stats, own, p, eh, el, blocks[4])
+    blocks[3], _ = lax.optimization_barrier((blocks[3], (up_sum, down_sum)))
+    part = sums(stats, own, p, eh, el, blocks[3])
     part = part + near_in[136:] + from_down + from_up
     coarse_centroids, top_centroids, _ = lax.optimization_barrier((coarse_centroids, top_centroids, up_sum))
     coarse_centers, top_centers = prepare(coarse_centroids), prepare(top_centroids)

time: 135 us -> 134 us (level)
    pallas_call x5 -> x4, Pallas kernels: 11.6 us -> 10.9 us  [sums(): pl.pallas_call(sums_kernel, grid_spec=pltpu.PrefetchScalarGridSpec(num_sc...]
where the time goes in v6:
time: 134 us
  blocking collectives  73.4 us (55%)
  Pallas kernels  27.9 us (21%)
  starting transfers between devices  20 us (15%)
  waiting for transfers between devices  10.5 us (8%)
    all_to_all x3, blocking collectives, spread(): lax.all_to_all(jnp.broadcast_to(value[None], (size, *value.shape)), axes,...  50.8 us
    all_to_all x1, blocking collectives, add_up(): return jnp.sum(lax.all_to_all(part, axes, 0, 0), axis=0)  13.2 us
    ppermute x5, starting transfers between devices, swap_core(): return lax.ppermute(value, 'c', [(0, 1), (1, 0)])  12 us
    pallas_call x4, Pallas kernels, sums(): pl.pallas_call(sums_kernel, grid_spec=pltpu.PrefetchScalarGridSpec(num_sc...  10.9 us
    pallas_call x1, Pallas kernels, fit(): pl.pallas_call(functools.partial(fit_kernel, step), in_specs=[pl.BlockSpe...  10.6 us
    all_to_all x1, blocking collectives, body(): lax.all_to_all(part.reshape(4, 17, 8, 128), 'zl', 0, 0)  9.39 us
    ppermute x4, waiting for transfers between devices, shift(): return lax.ppermute(value, 'x', [(i, (i + step) % 4) for i in range(4)])  5.4 us
    ppermute x4, starting transfers between devices, shift(): return lax.ppermute(value, 'x', [(i, (i + step) % 4) for i in range(4)])  5.27 us
  transfers between devices with their start and end apart: 12, of which 7 were waited for; matrix products, arithmetic and copies ran while one was open for 0% of the time, Pallas kernels for 8%

profile of v6, /device:TPU:1, one launch (start us, length us, event | category | flops | bytes accessed | tf_op | source)
XLA Modules:
  0.0 134.1 jit_solution(5629288326430327345)
XLA Ops:
  0.7 10.6 %fit.1 = (f32[512,2048]{1,0:T(8,128)S(1)}, f32[2,2048]{1,0:T(2,128)S(1)}, bf16[2048,1024]{1,0:T(8,128)(2,1)S(1)}, bf16[2048,1024]{1,0:T(8,128)(2,1)S(1)}) custom-call(f32[2048,1024]{1,0:T(8,128)} %e_hbm.1, f32[512,1024]{1,0:T(8,128)} %c_hbm.1), custom_call_target="tpu_custom_call" | custom-call | tf_op jit(solution)/shard_map/fit/pallas_call | solution.py:69
  11.3 0.1 pad_add_fusion.1._
  11.4 0.1 pad_add_fusion
  11.5 20.8 %all_to_all.25.stats_ref = f32[8,2,2048]{2,1,0:T(2,128)S(1)} all-to-all(f32[8,2,2048]{2,1,0:T(2,128)S(1)} %broadcast_in_dim.10), channel_id=1, replica_groups=mesh['x'=4,'zl'=4,'c'=2,'zh'=2,'y'=4] {'zh','y'}, dimensions={0} | all-to-all | bytes 262144 | tf_op jit(solution)/shard_map/all_to_all | solution.py:278
  32.3 2.8 %sums.4 = f32[136,8,128]{2,1,0:T(8,128)S(1)} custom-call(s32[2]{0:T(128)S(1)} %get-tuple-element.29._, f32[8,2,2048]{2,1,0:T(2,128)S(1)} %all_to_all.25.stats_ref, f32[2,2048]{1,0:T(2,128)S(1)} %get-tuple-element.30.own_ref, bf16[2048,1024]{1,0:T(8,128)(2,1)S(1)} %get-tuple-element.31.eh_ref, bf16[2048,1024]{1,0:T(8,128)(2,1)S(1)} %get-tuple-element.32.el_ref, ...), custom_call_target="tpu_custom_call" | custom-call | flops 1610612736 | bytes 8388608 | tf_op jit(solution)/shard_map/sums/pallas_call | solution.py:124
  35.1 2.2 %collective-permute-start = (f32[68,8,128]{2,1,0:T(8,128)S(1)}, f32[68,8,128]{2,1,0:T(8,128)S(1)}, u32[]{:S(2)}, u32[]{:S(2)}) collective-permute-start(f32[68,8,128]{2,1,0:T(8,128)S(1)} %slice.49), channel_id=1, source_target_pairs={{0,8},{8,0},{1,9},{9,1},{2,10},{10,2},{3,11},{11,3},{4,12},{12,4},... | collective-permute-start | bytes 835592 | tf_op jit(solution)/shard_map/ppermute | solution.py:287
  37.3 3.6 %sums.6 = f32[204,8,128]{2,1,0:T(8,128)S(1)} custom-call(s32[3]{0:T(128)S(1)} %pad_add_fusion.1._, f32[8,2,2048]{2,1,0:T(2,128)S(1)} %all_to_all.25.stats_ref, f32[2,2048]{1,0:T(2,128)S(1)} %get-tuple-element.30.own_ref, bf16[2048,1024]{1,0:T(8,128)(2,1)S(1)} %get-tuple-element.31.eh_ref, bf16[2048,1024]{1,0:T(8,128)(2,1)S(1)} %get-tuple-element.32.el_ref, ...), custom_call_target="tpu_custom_call" | custom-call | flops 2415919104 | bytes 8388608 | tf_op jit(solution)/shard_map/sums/pallas_call | solution.py:124
  40.9 0.1 collective-permute-start.1
  41.1 1.3 collective-permute-start.2
  42.4 1.5 %collective-permute-start.3 = (f32[34,8,128]{2,1,0:T(8,128)S(1)}, f32[34,8,128]{2,1,0:T(8,128)S(1)}, u32[]{:S(2)}, u32[]{:S(2)}) collective-permute-start(f32[34,8,128]{2,1,0:T(8,128)S(1)} %get-tuple-element.54), channel_id=1, source_target_pairs={{0,192},{64,0},{128,64},{192,128},{1,193},{65,1},{129,65},{193,129... | collective-permute-start | bytes 417800 | tf_op jit(solution)/shard_map/ppermute | solution.py:291
  43.9 2.8 %sums.5 = f32[136,8,128]{2,1,0:T(8,128)S(1)} custom-call(s32[2]{0:T(128)S(1)} %get-tuple-element.34._, f32[8,2,2048]{2,1,0:T(2,128)S(1)} %all_to_all.25.stats_ref, f32[2,2048]{1,0:T(2,128)S(1)} %get-tuple-element.30.own_ref, bf16[2048,1024]{1,0:T(8,128)(2,1)S(1)} %get-tuple-element.31.eh_ref, bf16[2048,1024]{1,0:T(8,128)(2,1)S(1)} %get-tuple-element.32.el_ref, ...), custom_call_target="tpu_custom_call" | custom-call | flops 1610612736 | bytes 8388608 | tf_op jit(solution)/shard_map/sums/pallas_call | solution.py:124
  46.7 0.0 copy-start.1
  46.7 0.0 copy-start
  46.7 0.0 collective-permute-done.1
  46.7 0.1 slice_add_fusion
  46.8 0.4 collective-permute-done.2
  47.2 0.0 collective-permute-done.3
  47.2 0.1 slice_add_fusion.4
  47.3 2.4 %collective-permute-start.5 = (f32[68,8,128]{2,1,0:T(8,128)S(1)}, f32[68,8,128]{2,1,0:T(8,128)S(1)}, u32[]{:S(2)}, u32[]{:S(2)}) collective-permute-start(f32[68,8,128]{2,1,0:T(8,128)S(1)} %pad_maximum_fusion.1), channel_id=1, source_target_pairs={{0,192},{64,0},{128,64},{192,128},{1,193},{65,1},{129,65},{193,129... | collective-permute-start | bytes 835592 | tf_op jit(solution)/shard_map/ppermute | solution.py:291
  49.7 0.1 collective-permute-start.4
  49.8 0.1 prepare.3.c_ref
  50.0 0.5 prepare.2.c_ref
  50.5 1.7 %sums.7 = f32[68,8,128]{2,1,0:T(8,128)S(1)} custom-call(s32[1]{0:T(128)} %bitcast.7._.slice_ref, f32[8,2,2048]{2,1,0:T(2,128)S(1)} %all_to_all.25.stats_ref, f32[2,2048]{1,0:T(2,128)S(1)} %get-tuple-element.30.own_ref, bf16[2048,1024]{1,0:T(8,128)(2,1)S(1)} %get-tuple-element.31.eh_ref, bf16[2048,1024]{1,0:T(8,128)(2,1)S(1)} %get-tuple-element.32.el_ref, ...), custom_call_target="tpu_custom_call" | custom-call | flops 805306368 | bytes 8388608 | tf_op jit(solution)/shard_map/sums/pallas_call | solution.py:124
  52.2 2.0 %collective-permute-done.5 = f32[68,8,128]{2,1,0:T(8,128)S(1)} collective-permute-done((f32[68,8,128]{2,1,0:T(8,128)S(1)}, f32[68,8,128]{2,1,0:T(8,128)S(1)}, u32[]{:S(2)}, u32[]{:S(2)}) %collective-permute-start.5) | collective-permute-done | bytes 278560 | tf_op jit(solution)/shard_map/ppermute | solution.py:291
  54.2 3.1 %collective-permute-done.4 = f32[68,8,128]{2,1,0:T(8,128)S(1)} collective-permute-done((f32[68,8,128]{2,1,0:T(8,128)S(1)}, f32[68,8,128]{2,1,0:T(8,128)S(1)}, u32[]{:S(2)}, u32[]{:S(2)}) %collective-permute-start.4) | collective-permute-done | bytes 278560 | tf_op jit(solution)/shard_map/ppermute | solution.py:291
  57.2 0.1 fusion.1
  57.3 9.4 %all_to_all.26.part_ref = f32[4,17,8,128]{3,2,1,0:T(8,128)S(1)} all-to-all(f32[4,17,8,128]{3,2,1,0:T(8,128)S(1)} %bitcast.14), channel_id=1, replica_groups=mesh['x'=4,'zl'=4,'c'=2,'zh'=2,'y'=4] {'zl'}, dimensions={0} | all-to-all | bytes 557056 | tf_op jit(solution)/shard_map/all_to_all | solution.py:337
  66.7 0.7 points.1
  67.4 1.5 %collective-permute-start.7 = (f32[16,1024]{1,0:T(8,128)S(1)}, f32[16,1024]{1,0:T(8,128)S(1)}, u32[]{:S(2)}, u32[]{:S(2)}) collective-permute-start(f32[16,1024]{1,0:T(8,128)S(1)} %get-tuple-element.42), channel_id=1, source_target_pairs={{0,192},{64,128},{128,64},{192,0},{1,193},{65,129},{129,65},{193,1... | collective-permute-start | bytes 196616 | tf_op jit(solution)/shard_map/ppermute | solution.py:296
  68.9 1.2 collective-permute-start.6
  70.1 1.9 %collective-permute-done.6 = f32[16,1024]{1,0:T(8,128)S(1)} collective-permute-done((f32[16,1024]{1,0:T(8,128)S(1)}, f32[16,1024]{1,0:T(8,128)S(1)}, u32[]{:S(2)}, u32[]{:S(2)}) %collective-permute-start.6) | collective-permute-done | bytes 65568 | tf_op jit(solution)/shard_map/ppermute | solution.py:296
  72.0 0.4 collective-permute-done.7
  72.5 5.4 %collective-permute-start.9 = (f32[64,1024]{1,0:T(8,128)S(1)}, f32[64,1024]{1,0:T(8,128)S(1)}, u32[]{:S(2)}, u32[]{:S(2)}) collective-permute-start(f32[64,1024]{1,0:T(8,128)S(1)} %constant_dynamic-update-slice_fusion.own_ref), channel_id=1, source_target_pairs={{0,8},{8,0},{1,9},{9,1},{2,10},{10,2},{3,11},{11,3},{4,12},{12,4},... | collective-permute-start | bytes 786440 | tf_op jit(solution)/shard_map/ppermute | solution.py:287
  77.9 1.2 collective-permute-done.9.other_ref
  79.1 1.7 %coarse.1 = f32[64,1152]{1,0:T(8,128)S(1)} custom-call(s32[1]{0:T(128)} %bitcast.7._.slice_ref, f32[64,1024]{1,0:T(8,128)S(1)} %constant_dynamic-update-slice_fusion.own_ref, f32[64,1024]{1,0:T(8,128)S(1)} %collective-permute-done.9.other_ref, bf16[1024,1024]{1,0:T(8,128)(2,1)S(1)} %prepare.2.c_ref), custom_call_target="tpu_custom_call" | custom-call | tf_op jit(solution)/shard_map/coarse/pallas_call | solution.py:209
  80.7 0.2 reshape.25
  80.9 13.2 %all_to_all.27 = f32[32,2,1152]{2,1,0:T(2,128)S(1)} all-to-all(f32[32,2,1152]{2,1,0:T(2,128)S(1)} %reshape.25), channel_id=1, replica_groups=mesh['x'=4,'zl'=4,'c'=2,'zh'=2,'y'=4] {'y','zh','zl'}, dimensions={0} | all-to-all | bytes 589824 | tf_op jit(solution)/shard_map/all_to_all | solution.py:283
  94.2 0.1 reduce_sum.9
  94.3 0.1 slice_reduce_fusion
  94.4 0.1 slice_divide_fusion
  94.5 11.9 %all_to_all.28 = f32[8,2,1024]{2,1,0:T(2,128)S(1)} all-to-all(f32[8,2,1024]{2,1,0:T(2,128)S(1)} %broadcast_in_dim.24), channel_id=1, replica_groups=mesh['x'=4,'zl'=4,'c'=2,'zh'=2,'y'=4] {'zh','zl'}, dimensions={0} | all-to-all | bytes 131072 | tf_op jit(solution)/shard_map/all_to_all | solution.py:278
  106.5 0.1 broadcast_in_dim.26
  106.6 18.1 %all_to_all.29 = f32[16,16,1024]{2,1,0:T(8,128)S(1)} all-to-all(f32[16,16,1024]{2,1,0:T(8,128)S(1)} %broadcast_in_dim.26), channel_id=1, replica_groups=mesh['x'=4,'zl'=4,'c'=2,'zh'=2,'y'=4] {'x','y'}, dimensions={0} | all-to-all | bytes 2097152 | tf_op jit(solution)/shard_map/all_to_all | solution.py:278
  124.7 4.2 %collective-permute-start.10 = (f32[256,1024]{1,0:T(8,128)S(1)}, f32[256,1024]{1,0:T(8,128)S(1)}, u32[]{:S(2)}, u32[]{:S(2)}) collective-permute-start(f32[256,1024]{1,0:T(8,128)S(1)} %bitcast.12), channel_id=1, source_target_pairs={{0,8},{8,0},{1,9},{9,1},{2,10},{10,2},{3,11},{11,3},{4,12},{12,4},... | collective-permute-start | bytes 3145736 | tf_op jit(solution)/shard_map/ppermute | solution.py:287
  128.9 1.6 %top.1 = (f32[64,1152]{1,0:T(8,128)S(1)}, f32[512,1024]{1,0:T(8,128)}) custom-call(s32[1]{0:T(128)} %bitcast.10.core_ref, f32[256,1024]{1,0:T(8,128)S(1)} %bitcast.13, bf16[128,1024]{1,0:T(8,128)(2,1)S(1)} %prepare.3.c_ref), custom_call_target="tpu_custom_call" | custom-call | tf_op jit(solution)/shard_map/top/pallas_call | solution.py:237
  130.5 0.1 collective-permute-start.11
  130.6 1.6 %collective-permute-done.11.add_ref = f32[64,1152]{1,0:T(8,128)S(1)} collective-permute-done((f32[64,1152]{1,0:T(8,128)S(1)}, f32[64,1152]{1,0:T(8,128)S(1)}, u32[]{:S(2)}, u32[]{:S(2)}) %collective-permute-start.11) | collective-permute-done | bytes 294944 | tf_op jit(solution)/shard_map/ppermute | solution.py:287
  132.2 1.7 %final.1 = (f32[512,1024]{1,0:T(8,128)}, f32[64,1024]{1,0:T(8,128)}) custom-call(s32[1]{0:T(128)} %bitcast.10.core_ref, f32[512,1024]{1,0:T(8,128)} %get-tuple-element.45._, f32[256,1024]{1,0:T(8,128)S(1)} %collective-permute-done.10.other_ref, f32[64,1152]{1,0:T(8,128)S(1)} %get-tuple-element.46.part_ref, ...), custom_call_target="tpu_custom_call", output_to_operand_aliasing={{0}: (1, {})} | custom-call | tf_op jit(solution)/shard_map/final/pallas_call | solution.py:262
  (18 shorter events, 0.3 us)
Async XLA Ops:
  35.1 6.0 %collective-permute-start = (f32[68,8,128]{2,1,0:T(8,128)S(1)}, f32[68,8,128]{2,1,0:T(8,128)S(1)}, u32[]{:S(2)}, u32[]{:S(2)}) collective-permute-start(f32[68,8,128]{2,1,0:T(8,128)S(1)} %slice.49), channel_id=1, source_target_pairs={{0,8},{8,0},{1,9},{9,1},{2,10},{10,2},{3,11},{11,3},{4,12},{12,4},... | collective-permute-start | bytes 835592 | tf_op jit(solution)/shard_map/ppermute | solution.py:287
  40.9 5.8 %collective-permute-start.1 = (f32[204,8,128]{2,1,0:T(8,128)S(1)}, f32[204,8,128]{2,1,0:T(8,128)S(1)}, u32[]{:S(2)}, u32[]{:S(2)}) collective-permute-start(f32[204,8,128]{2,1,0:T(8,128)S(1)} %sums.6), channel_id=1, source_target_pairs={{0,8},{8,0},{1,9},{9,1},{2,10},{10,2},{3,11},{11,3},{4,12},{12,4},... | collective-permute-start | bytes 2506760 | tf_op jit(solution)/shard_map/ppermute | solution.py:287
  41.1 6.0 %collective-permute-start.2 = (f32[34,8,128]{2,1,0:T(8,128)S(1)}, f32[34,8,128]{2,1,0:T(8,128)S(1)}, u32[]{:S(2)}, u32[]{:S(2)}) collective-permute-start(f32[34,8,128]{2,1,0:T(8,128)S(1)} %get-tuple-element.53), channel_id=1, source_target_pairs={{0,64},{64,128},{128,192},{192,0},{1,65},{65,129},{129,193},{193,1... | collective-permute-start | bytes 417800 | tf_op jit(solution)/shard_map/ppermute | solution.py:291
  42.4 4.8 %collective-permute-start.3 = (f32[34,8,128]{2,1,0:T(8,128)S(1)}, f32[34,8,128]{2,1,0:T(8,128)S(1)}, u32[]{:S(2)}, u32[]{:S(2)}) collective-permute-start(f32[34,8,128]{2,1,0:T(8,128)S(1)} %get-tuple-element.54), channel_id=1, source_target_pairs={{0,192},{64,0},{128,64},{192,128},{1,193},{65,1},{129,65},{193,129... | collective-permute-start | bytes 417800 | tf_op jit(solution)/shard_map/ppermute | solution.py:291
  46.7 3.1 %copy-start.1 = (f32[64,1024]{1,0:T(8,128)S(1)}, f32[64,1024]{1,0:T(8,128)}, u32[]{:S(2)}) copy-start(f32[64,1024]{1,0:T(8,128)} %c_ref.1) | copy-start | bytes 786436
  46.7 3.3 %copy-start = (f32[512,1024]{1,0:T(8,128)S(1)}, f32[512,1024]{1,0:T(8,128)}, u32[]{:S(2)}) copy-start(f32[512,1024]{1,0:T(8,128)} %c_ref) | copy-start | bytes 6291460
  47.3 6.9 %collective-permute-start.5 = (f32[68,8,128]{2,1,0:T(8,128)S(1)}, f32[68,8,128]{2,1,0:T(8,128)S(1)}, u32[]{:S(2)}, u32[]{:S(2)}) collective-permute-start(f32[68,8,128]{2,1,0:T(8,128)S(1)} %pad_maximum_fusion.1), channel_id=1, source_target_pairs={{0,192},{64,0},{128,64},{192,128},{1,193},{65,1},{129,65},{193,129... | collective-permute-start | bytes 835592 | tf_op jit(solution)/shard_map/ppermute | solution.py:291
  49.7 7.5 %collective-permute-start.4 = (f32[68,8,128]{2,1,0:T(8,128)S(1)}, f32[68,8,128]{2,1,0:T(8,128)S(1)}, u32[]{:S(2)}, u32[]{:S(2)}) collective-permute-start(f32[68,8,128]{2,1,0:T(8,128)S(1)} %pad_maximum_fusion), channel_id=1, source_target_pairs={{0,64},{64,128},{128,192},{192,0},{1,65},{65,129},{129,193},{193,1... | collective-permute-start | bytes 835592 | tf_op jit(solution)/shard_map/ppermute | solution.py:291
  67.4 5.0 %collective-permute-start.8 = (f32[16,1024]{1,0:T(8,128)S(1)}, f32[16,1024]{1,0:T(8,128)S(1)}, u32[]{:S(2)}, u32[]{:S(2)}) collective-permute-start(f32[16,1024]{1,0:T(8,128)S(1)} %get-tuple-element.42), channel_id=1, source_target_pairs={{0,128},{64,192},{128,0},{192,64},{1,129},{65,193},{129,1},{193,65... | collective-permute-start | bytes 196616 | tf_op jit(solution)/shard_map/ppermute | solution.py:296
  67.4 5.0 %collective-permute-start.7 = (f32[16,1024]{1,0:T(8,128)S(1)}, f32[16,1024]{1,0:T(8,128)S(1)}, u32[]{:S(2)}, u32[]{:S(2)}) collective-permute-start(f32[16,1024]{1,0:T(8,128)S(1)} %get-tuple-element.42), channel_id=1, source_target_pairs={{0,192},{64,128},{128,64},{192,0},{1,193},{65,129},{129,65},{193,1... | collective-permute-start | bytes 196616 | tf_op jit(solution)/shard_map/ppermute | solution.py:296
  68.9 3.1 %collective-permute-start.6 = (f32[16,1024]{1,0:T(8,128)S(1)}, f32[16,1024]{1,0:T(8,128)S(1)}, u32[]{:S(2)}, u32[]{:S(2)}) collective-permute-start(f32[16,1024]{1,0:T(8,128)S(1)} %get-tuple-element.42), channel_id=1, source_target_pairs={{0,64},{64,0},{128,192},{192,128},{1,65},{65,1},{129,193},{193,129... | collective-permute-start | bytes 196616 | tf_op jit(solution)/shard_map/ppermute | solution.py:296
  72.5 6.6 %collective-permute-start.9 = (f32[64,1024]{1,0:T(8,128)S(1)}, f32[64,1024]{1,0:T(8,128)S(1)}, u32[]{:S(2)}, u32[]{:S(2)}) collective-permute-start(f32[64,1024]{1,0:T(8,128)S(1)} %constant_dynamic-update-slice_fusion.own_ref), channel_id=1, source_target_pairs={{0,8},{8,0},{1,9},{9,1},{2,10},{10,2},{3,11},{11,3},{4,12},{12,4},... | collective-permute-start | bytes 786440 | tf_op jit(solution)/shard_map/ppermute | solution.py:287
  124.7 7.5 %collective-permute-start.10 = (f32[256,1024]{1,0:T(8,128)S(1)}, f32[256,1024]{1,0:T(8,128)S(1)}, u32[]{:S(2)}, u32[]{:S(2)}) collective-permute-start(f32[256,1024]{1,0:T(8,128)S(1)} %bitcast.12), channel_id=1, source_target_pairs={{0,8},{8,0},{1,9},{9,1},{2,10},{10,2},{3,11},{11,3},{4,12},{12,4},... | collective-permute-start | bytes 3145736 | tf_op jit(solution)/shard_map/ppermute | solution.py:287
  130.5 1.7 %collective-permute-start.11 = (f32[64,1152]{1,0:T(8,128)S(1)}, f32[64,1152]{1,0:T(8,128)S(1)}, u32[]{:S(2)}, u32[]{:S(2)}) collective-permute-start(f32[64,1152]{1,0:T(8,128)S(1)} %get-tuple-element.46.part_ref), channel_id=1, source_target_pairs={{0,8},{8,0},{1,9},{9,1},{2,10},{10,2},{3,11},{11,3},{4,12},{12,4},... | collective-permute-start | bytes 884744 | tf_op jit(solution)/shard_map/ppermute | solution.py:287
